TPU v7x, 32 devices: a whole 2x2x4 slice. The times are simulated.
32 devices in a mesh: row: 8 (over z, core), col: 4 (over y, x).
Axes of the slice: x: 2, y: 2, z: 4, core: 2. Of those that a mesh axis runs over, the one named last changes fastest.
Arguments:
- tokens: bfloat16 [4096, 1024], P('row', 'col')
- cotangent: bfloat16 [4096, 1024], P('row', 'col'), may hold values from -6 to 6
- deal_order: int32 [4096], replicated, may hold values from 0 to 4095, as said below
- seq_lengths: int32 [8, 4], P('row'), may hold values from 1 to 256, 512 in all within a row
- value_picks: int32 [4096, 4, 32], P('row'), may hold values from 0 to 65535
- norm1_gain: float32 [1024], P('col'), may hold values from 0.5 to 1.5
- w_qkv: float32 [1024, 3072], P('row', 'col'), may hold values from -0.1875 to 0.1875
- w_attn_out: float32 [1024, 1024], P('col', 'row'), may hold values from -3 to 3
- norm2_gain: float32 [1024], P('col'), may hold values from 0.5 to 1.5
- w_query: float32 [1024, 4096], P('row', 'col'), may hold values from -0.1875 to 0.1875
- sub_keys: float32 [8, 256, 512], P('col', 'row'), may hold values from -0.09375 to 0.09375
- value_table: float32 [65536, 1024], P('row', 'col'), may hold values from -6 to 6
- w_gate: float32 [1024, 1024], P('row', 'col'), may hold values from -0.1875 to 0.1875
- w_mem_out: float32 [1024, 1024], P('col', 'row'), may hold values from -0.75 to 0.75
Outputs:
- output: float32 [4096, 1024], P('row', 'col')
- grad_tokens: float32 [4096, 1024], P('row', 'col')
- grad_norm1_gain: float32 [1024], P(('col', 'row'))
- grad_w_qkv: float32 [1024, 3072], P('row', 'col')
- grad_w_attn_out: float32 [1024, 1024], P('col', 'row')
- grad_norm2_gain: float32 [1024], P(('col', 'row'))
- grad_w_query: float32 [1024, 4096], P('row', 'col')
- grad_sub_keys: float32 [8, 256, 512], P('col', 'row')
- grad_value_table: float32 [65536, 1024], P('row', 'col')
- grad_w_gate: float32 [1024, 1024], P('row', 'col')
- grad_w_mem_out: float32 [1024, 1024], P('col', 'row')
Inputs may be any that keep to these rules, and one draw needn't show every extreme that they name: Dealt slot s holds initial token deal_order[s], each token once. Of the 512 tokens of one aligned block of initial positions, at most 128 go to any one aligned block of 512 dealt slots, and exactly 128 go to some block. `seq_lengths`: each row sums to 512. `value_picks`: row i of the memory pairs first-half sub-key i // 256 with second-half sub-key i % 256.
All inputs are finite; a program needn't handle non-finite values.
Results may differ from a plain program's by a relative error of at most 0.0095.
The roundings to bfloat16 on the way count: a program that leaves them out, or rounds other values in their place, can miss the bound.
Values may be sent and summed in bfloat16 or wider, within the bound.
A program may use at most 384 MiB of HBM per device.

v0:
```python
import jax
import jax.numpy as jnp
from jax import lax
from jax.sharding import PartitionSpec as P

D = 1024
HD = 64
MH = 4
QD = 512
NK = 256
PICKS = 32


EPS = 1e-05
MASKED = -1e30


def pack_rows(values, positions, slot_count):
    buffer = jnp.zeros((slot_count,) + values.shape[1:], values.dtype)
    return buffer.at[positions].set(values)


def norm_forward(values, gain):
    factor = lax.rsqrt(jnp.mean(values * values, axis=1, keepdims=True) + EPS)
    return (factor, (values * factor * gain.astype(jnp.float32)).astype(jnp.bfloat16))


def norm_backward(values, factor, gain, grad_hidden):
    scaled = grad_hidden * gain.astype(jnp.float32)
    inner = jnp.sum(scaled * values, axis=1, keepdims=True)
    grad_values = factor * scaled - values * (factor * factor * factor) * inner / D
    grad_gain = jnp.sum(grad_hidden * values * factor, axis=0)
    return (grad_values, grad_gain)


def allowed_mask(seq_ids, start_row, block_len):
    places = jnp.arange(seq_ids.shape[0], dtype=jnp.int32)
    query_pos = start_row + jnp.arange(block_len, dtype=jnp.int32)
    return (seq_ids[:, None] == seq_ids[None, :]) & (query_pos[:, None] >= places[None, :])


def scatter_picks(accum, base_row, weights_low, grads_low, picks):
    span = accum.shape[0]
    width = accum.shape[1]
    rows = picks.shape[0]

    def add_block(total, start_blk):
        pick_blk = picks - base_row
        inside = (pick_blk >= 0) & (pick_blk < span)
        target = jnp.where(inside, pick_blk, span)
        weight_blk = weights_low.astype(jnp.float32)
        grad_blk = grads_low.astype(jnp.float32)
        update = weight_blk[:, :, None] * grad_blk[:, None, :]
        return (total.at[target.reshape(-1)].add(update.reshape(-1, width), mode="drop"), None)

    starts = jnp.arange(rows // rows, dtype=jnp.int32) * rows
    total, unused = lax.scan(add_block, accum, starts)
    return total


def attention_forward(queries, key_rows, value_rows, seq_ids, score_scale):
    tok_rows = queries.shape[0]

    def one_block(start_row):
        scores = (
            jnp.einsum("qhd,khd->hqk", queries, key_rows, preferred_element_type=jnp.float32)
            * score_scale
        )
        scores = jnp.where(allowed_mask(seq_ids, start_row, tok_rows)[None], scores, MASKED)
        row_max = jnp.max(scores, axis=2, keepdims=True)
        shifted_exp = jnp.exp(scores - row_max)
        row_total = jnp.sum(shifted_exp, axis=2, keepdims=True)
        weights_low = (shifted_exp / row_total).astype(jnp.bfloat16)
        weighted = jnp.einsum(
            "hqk,khd->qhd", weights_low, value_rows, preferred_element_type=jnp.float32
        )
        return (weighted.astype(jnp.bfloat16), (row_max + jnp.log(row_total))[:, :, 0])

    starts = jnp.arange(tok_rows // tok_rows, dtype=jnp.int32) * tok_rows
    weighted, log_total = lax.map(one_block, starts)
    return (weighted.reshape(tok_rows, queries.shape[1] * queries.shape[2]), log_total)


def attention_backward(queries, key_rows, value_rows, grad_out, log_total, seq_ids, score_scale):
    tok_rows = queries.shape[0]

    def one_block(carry, inputs):
        key_grad, value_grad = carry
        start_row, log_blk = inputs
        scores = (
            jnp.einsum("qhd,khd->hqk", queries, key_rows, preferred_element_type=jnp.float32)
            * score_scale
        )
        scores = jnp.where(allowed_mask(seq_ids, start_row, tok_rows)[None], scores, MASKED)
        probs = jnp.exp(scores - log_blk[:, :, None])
        grad_prob = jnp.einsum(
            "qhd,khd->hqk", grad_out, value_rows, preferred_element_type=jnp.float32
        )
        inner = jnp.sum(probs * grad_prob, axis=2, keepdims=True)
        grad_score = (probs * (grad_prob - inner)).astype(jnp.bfloat16)
        query_grad = (
            jnp.einsum("hqk,khd->qhd", grad_score, key_rows, preferred_element_type=jnp.float32)
            * score_scale
        )
        key_grad = (
            key_grad
            + jnp.einsum("hqk,qhd->khd", grad_score, queries, preferred_element_type=jnp.float32)
            * score_scale
        )
        value_grad = value_grad + jnp.einsum(
            "hqk,qhd->khd", probs.astype(jnp.bfloat16), grad_out, preferred_element_type=jnp.float32
        )
        return ((key_grad, value_grad), query_grad)

    starts = jnp.arange(tok_rows // tok_rows, dtype=jnp.int32) * tok_rows
    zeros_like = jnp.zeros(queries.shape, jnp.float32)
    (key_grad, value_grad), query_grad = lax.scan(
        one_block, (zeros_like, zeros_like), (starts, log_total)
    )
    return (query_grad.reshape(queries.shape), key_grad, value_grad)


def per_device(
    tokens,
    cotangent,
    deal_order,
    seq_lengths,
    value_picks,
    norm1_gain,
    w_qkv,
    w_attn_out,
    norm2_gain,
    w_query,
    sub_keys,
    value_table,
    w_gate,
    w_mem_out,
):
    row_count = lax.axis_size("row")
    row_index = lax.axis_index("row")
    col_index = lax.axis_index("col")
    tok_rows = tokens.shape[0]
    col_width = tokens.shape[1]
    capacity = 2 * tok_rows // row_count
    slot_count = row_count * capacity
    all_rows = deal_order.shape[0]
    my_first = row_index * tok_rows
    my_slots = lax.dynamic_slice_in_dim(deal_order, my_first, tok_rows)
    source_dev = my_slots // tok_rows
    device_ids = jnp.arange(row_count, dtype=jnp.int32)
    from_source = (source_dev[:, None] == device_ids[None, :]).astype(jnp.int32)
    earlier = jnp.cumsum(from_source, axis=0) - from_source
    recv_pos = source_dev * capacity + jnp.sum(earlier * from_source, axis=1)
    owned = (deal_order // tok_rows == row_index).astype(jnp.int32).reshape(row_count, tok_rows)
    rank_all = (jnp.cumsum(owned, axis=1) - owned).reshape(all_rows)
    inverse = (
        jnp.zeros((all_rows,), jnp.int32).at[deal_order].set(jnp.arange(all_rows, dtype=jnp.int32))
    )
    dest_slot = lax.dynamic_slice_in_dim(inverse, my_first, tok_rows)
    send_pos = dest_slot // tok_rows * capacity + rank_all[dest_slot]
    got_tokens, got_cot = (
        lax.all_to_all(
            pack_rows(tokens, send_pos, slot_count), "row", split_axis=0, concat_axis=0, tiled=True
        ),
        lax.all_to_all(
            pack_rows(cotangent, send_pos, slot_count),
            "row",
            split_axis=0,
            concat_axis=0,
            tiled=True,
        ),
    )
    full_tokens, full_cot, gain_one, gain_two = (
        lax.all_gather(got_tokens[recv_pos], "col", axis=1, tiled=True),
        lax.all_gather(got_cot[recv_pos], "col", axis=1, tiled=True),
        lax.all_gather(norm1_gain.astype(jnp.bfloat16), "col", axis=0, tiled=True),
        lax.all_gather(norm2_gain.astype(jnp.bfloat16), "col", axis=0, tiled=True),
    )
    qkv_weight, query_weight, gate_weight, attn_weight, memout_weight, key_table = (
        lax.all_gather(w_qkv.astype(jnp.bfloat16), "row", axis=0, tiled=True),
        lax.all_gather(w_query.astype(jnp.bfloat16), "row", axis=0, tiled=True),
        lax.all_gather(w_gate.astype(jnp.bfloat16), "row", axis=0, tiled=True),
        lax.all_gather(w_attn_out.astype(jnp.bfloat16), "row", axis=1, tiled=True),
        lax.all_gather(w_mem_out.astype(jnp.bfloat16), "row", axis=1, tiled=True),
        lax.all_gather(sub_keys.astype(jnp.bfloat16), "row", axis=1, tiled=True),
    )
    table_rows = lax.all_gather(value_table.astype(jnp.bfloat16), "row", axis=0, tiled=True)
    heads_here = col_width // HD
    halves_here = query_weight.shape[1] // QD
    score_scale = HD ** (-0.5)
    seq_ids = jnp.sum(
        (
            jnp.arange(tok_rows, dtype=jnp.int32)[:, None] >= jnp.cumsum(seq_lengths[0])[None, :]
        ).astype(jnp.int32),
        axis=1,
    )
    starts = jnp.arange(tok_rows // tok_rows, dtype=jnp.int32) * tok_rows
    dealt_x = full_tokens.astype(jnp.float32)
    factor_one, hidden_one = norm_forward(dealt_x, gain_one)
    qkv = (
        jnp.dot(hidden_one, qkv_weight, preferred_element_type=jnp.float32)
        .astype(jnp.bfloat16)
        .reshape(tok_rows, heads_here, 3, HD)
    )
    queries = qkv[:, :, 0, :]
    key_rows = qkv[:, :, 1, :]
    value_rows = qkv[:, :, 2, :]
    mixed, log_total = attention_forward(queries, key_rows, value_rows, seq_ids, score_scale)
    attn_part = jnp.dot(mixed, attn_weight, preferred_element_type=jnp.float32)
    resid = dealt_x + lax.psum(attn_part, "col")
    factor_two, hidden_two = norm_forward(resid, gain_two)
    mem_queries = (
        jnp.dot(hidden_two, query_weight, preferred_element_type=jnp.float32)
        .astype(jnp.bfloat16)
        .reshape(tok_rows, halves_here, QD)
    )
    sub_scores = jnp.einsum(
        "tnq,njq->tnj", mem_queries, key_table, preferred_element_type=jnp.float32
    )
    half_ids = col_index * halves_here + jnp.arange(halves_here, dtype=jnp.int32)
    head_ids = half_ids // 2
    my_picks = jnp.take(value_picks, head_ids, axis=1)
    sub_index = jnp.where((half_ids % 2 == 0)[None, :, None], my_picks // NK, my_picks % NK)
    key_ids = jnp.arange(NK, dtype=jnp.int32)

    def pick_partial(start_row):
        match = sub_index[..., None] == key_ids
        return jnp.sum(jnp.where(match, sub_scores[:, :, None, :], 0.0), axis=3)

    partial_value = lax.map(pick_partial, starts).reshape(tok_rows, halves_here * PICKS)
    gathered = lax.all_gather(partial_value, "col", axis=1, tiled=True)
    score = jnp.sum(gathered.reshape(tok_rows, MH, 2, PICKS), axis=2)
    pick_weights = jax.nn.softmax(score, axis=-1).reshape(tok_rows, MH * PICKS)
    pick_weights_low = pick_weights.astype(jnp.bfloat16)
    picks_flat = value_picks.reshape(tok_rows, MH * PICKS)

    def read_memory(start_row):
        return jnp.einsum(
            "tp,tpd->td",
            pick_weights_low,
            table_rows[picks_flat],
            preferred_element_type=jnp.float32,
        )

    memory = lax.map(read_memory, starts).reshape(tok_rows, col_width)
    gate = jnp.dot(hidden_two, gate_weight, preferred_element_type=jnp.float32)
    sigmoid_gate = jax.nn.sigmoid(gate)
    mixed_two = (memory * gate * sigmoid_gate).astype(jnp.bfloat16)
    memout_part = jnp.dot(mixed_two, memout_weight, preferred_element_type=jnp.float32)
    memory_out = lax.psum_scatter(
        memout_part.astype(jnp.bfloat16), "col", scatter_dimension=1, tiled=True
    ).astype(jnp.float32)
    result_block = lax.dynamic_slice_in_dim(resid, col_index * col_width, col_width, 1) + memory_out
    grad_mixed_two = jnp.einsum(
        "tD,cD->tc", full_cot, memout_weight, preferred_element_type=jnp.float32
    )
    grad_memout_w = jnp.einsum("tc,tD->cD", mixed_two, full_cot, preferred_element_type=jnp.float32)
    grad_memory = (grad_mixed_two * gate * sigmoid_gate).astype(jnp.bfloat16)
    grad_gate = (
        grad_mixed_two * memory * sigmoid_gate * (1.0 + gate * (1.0 - sigmoid_gate))
    ).astype(jnp.bfloat16)
    grad_gate_w = jnp.einsum("tD,tc->Dc", hidden_two, grad_gate, preferred_element_type=jnp.float32)
    table_back = lax.all_gather(value_table.astype(jnp.bfloat16), "row", axis=0, tiled=True)

    def pick_grad(start_row):
        return jnp.einsum(
            "td,tpd->tp", grad_memory, table_back[picks_flat], preferred_element_type=jnp.float32
        )

    grad_weight_pick = lax.psum(lax.map(pick_grad, starts).reshape(tok_rows, MH * PICKS), "col")
    weights_grouped = pick_weights.reshape(tok_rows, MH, PICKS)
    pick_grad_grouped = grad_weight_pick.reshape(tok_rows, MH, PICKS)
    grad_score = weights_grouped * (
        pick_grad_grouped - jnp.sum(weights_grouped * pick_grad_grouped, axis=2, keepdims=True)
    )
    grad_score_mine = jnp.take(grad_score, head_ids, axis=1)

    def sub_grad(start_row):
        match = sub_index[..., None] == key_ids
        return jnp.sum(jnp.where(match, grad_score_mine[..., None], 0.0), axis=2)

    grad_sub = lax.map(sub_grad, starts).reshape(tok_rows, halves_here, NK).astype(jnp.bfloat16)
    grad_queries = (
        jnp.einsum("tnj,njq->tnq", grad_sub, key_table, preferred_element_type=jnp.float32)
        .astype(jnp.bfloat16)
        .reshape(tok_rows, halves_here * QD)
    )
    grad_keys = jnp.einsum(
        "tnj,tnq->njq", grad_sub, mem_queries, preferred_element_type=jnp.float32
    )
    grad_query_w = jnp.einsum(
        "tD,tm->Dm", hidden_two, grad_queries, preferred_element_type=jnp.float32
    )
    hidden_two_part = jnp.einsum(
        "tm,Dm->tD", grad_queries, query_weight, preferred_element_type=jnp.float32
    ) + jnp.einsum("tc,Dc->tD", grad_gate, gate_weight, preferred_element_type=jnp.float32)
    grad_hidden_two = lax.psum(hidden_two_part, "col")
    grad_resid, grad_gain_two = norm_backward(resid, factor_two, gain_two, grad_hidden_two)
    grad_resid = grad_resid + full_cot.astype(jnp.float32)
    grad_attn_low = grad_resid.astype(jnp.bfloat16)
    grad_mixed = (
        jnp.einsum("tD,cD->tc", grad_attn_low, attn_weight, preferred_element_type=jnp.float32)
        .astype(jnp.bfloat16)
        .reshape(tok_rows, heads_here, HD)
    )
    grad_attn_w = jnp.einsum("tc,tD->cD", mixed, grad_attn_low, preferred_element_type=jnp.float32)
    query_grad, key_grad, value_grad = attention_backward(
        queries, key_rows, value_rows, grad_mixed, log_total, seq_ids, score_scale
    )
    grad_qkv = (
        jnp.stack((query_grad, key_grad, value_grad), axis=2)
        .astype(jnp.bfloat16)
        .reshape(tok_rows, heads_here * 3 * HD)
    )
    grad_qkv_w = jnp.einsum("tD,tm->Dm", hidden_one, grad_qkv, preferred_element_type=jnp.float32)
    hidden_one_part = jnp.einsum(
        "tm,Dm->tD", grad_qkv, qkv_weight, preferred_element_type=jnp.float32
    )
    grad_hidden_one = lax.psum(hidden_one_part, "col")
    grad_dealt, grad_gain_one = norm_backward(dealt_x, factor_one, gain_one, grad_hidden_one)
    grad_dealt = grad_dealt + grad_resid
    grad_block = lax.dynamic_slice_in_dim(grad_dealt, col_index * col_width, col_width, 1)
    gain_one_block = lax.dynamic_slice_in_dim(grad_gain_one, col_index * col_width, col_width)
    gain_two_block = lax.dynamic_slice_in_dim(grad_gain_two, col_index * col_width, col_width)
    grads = (
        lax.psum_scatter(grad_qkv_w, "row", scatter_dimension=0, tiled=True),
        lax.psum_scatter(grad_query_w, "row", scatter_dimension=0, tiled=True),
        lax.psum_scatter(grad_gate_w, "row", scatter_dimension=0, tiled=True),
        lax.psum_scatter(grad_attn_w, "row", scatter_dimension=1, tiled=True),
        lax.psum_scatter(grad_memout_w, "row", scatter_dimension=1, tiled=True),
        lax.psum_scatter(grad_keys, "row", scatter_dimension=1, tiled=True),
        lax.psum_scatter(gain_one_block, "row", scatter_dimension=0, tiled=True),
        lax.psum_scatter(gain_two_block, "row", scatter_dimension=0, tiled=True),
    )
    own_rows = value_table.shape[0]
    table_total = scatter_picks(
        jnp.zeros((own_rows * row_count, col_width), jnp.float32),
        0,
        pick_weights_low,
        grad_memory,
        picks_flat,
    )
    grad_table = lax.psum_scatter(table_total, "row", scatter_dimension=0, tiled=True)
    got_result, got_grad = (
        lax.all_to_all(
            pack_rows(result_block, recv_pos, slot_count),
            "row",
            split_axis=0,
            concat_axis=0,
            tiled=True,
        ),
        lax.all_to_all(
            pack_rows(grad_block, recv_pos, slot_count),
            "row",
            split_axis=0,
            concat_axis=0,
            tiled=True,
        ),
    )
    return (
        got_result[send_pos],
        got_grad[send_pos],
        grads[6],
        grads[0],
        grads[3],
        grads[7],
        grads[1],
        grads[5],
        grad_table,
        grads[2],
        grads[4],
    )


def solution(mesh):
    return jax.shard_map(
        per_device,
        mesh=mesh,
        in_specs=(
            P("row", "col"),
            P("row", "col"),
            P(),
            P("row", None),
            P("row", None, None),
            P("col"),
            P("row", "col"),
            P("col", "row"),
            P("col"),
            P("row", "col"),
            P("col", "row", None),
            P("row", "col"),
            P("row", "col"),
            P("col", "row"),
        ),
        out_specs=(
            P("row", "col"),
            P("row", "col"),
            P(("col", "row")),
            P("row", "col"),
            P("col", "row"),
            P(("col", "row")),
            P("row", "col"),
            P("col", "row", None),
            P("row", "col"),
            P("row", "col"),
            P("col", "row"),
        ),
        check_vma=False,
    )
```

profile of v0, /device:TPU:0, one launch (start us, length us, event | category | flops | bytes accessed | tf_op | source)
XLA Modules:
  0.0 3228.9 jit_solution(2876433636481066471)
XLA Ops:
  10.9 15.5 scatter_custom_fusion
  26.5 3.1 gather_fusion
  29.8 3.6 scatter_custom_fusion.1
  33.3 6.5 all-to-all-start
  43.7 11.5 all-to-all-done
  55.2 2.6 gather_fusion.1
  58.8 8.1 all-gather.2
  67.0 14.0 all_gather.40
  81.2 2.1 all-gather.16.cloned.1.call-done
  83.3 1.5 fusion.11
  85.4 25.2 all-gather.10.cloned.1.call-done
  110.6 2.8 convolution_convert_fusion.3
  117.5 1.8 fusion.105
  120.7 5.8 convert_element_type.168
  126.5 3.7 scatter_custom_fusion.3
  130.2 3.5 all-to-all-start.2
  133.8 8.0 all-gather.3
  144.7 15.1 all_gather.47
  159.8 15.8 all_gather.46
  175.6 15.9 all_gather.43
  191.5 2.6 gather_fusion.5
  194.2 1.9 multiply_reduce_fusion.3
  199.2 20.8 all-gather.12.cloned.1.call-done
  219.9 3.2 convolution_convert_fusion.2
  225.5 11.5 select_reduce_fusion.1
  238.3 11.6 all_gather.44
  252.0 258.2 %all-gather.14.cloned.1.call-done = bf16[65536,256]{1,0:T(8,128)(2,1)} async-done(((bf16[8192,256]{1,0:T(8,128)(2,1)}), bf16[65536,256]{1,0:T(8,128)(2,1)}) %all-gather.14.cloned.1.call-update) | async-done | bytes 33554448 | tf_op jit(solution)/shard_map/all_gather | solution.py:187
  510.2 992.7 %gather_fusion.3 = bf16[65536,256]{1,0:T(8,128)(2,1)} fusion(bf16[65536,256]{1,0:T(8,128)(2,1)} %all-gather.14.cloned.1.call-done, s32[65536]{0:T(1024)} %bitcast_clamp_fusion), kind=kCustom, calls=%fused_computation.3 | custom fusion | bytes 67371008 | tf_op jit(solution)/shard_map/while/body/eval_jaxpr/gather | solution.py:241
  1502.9 13.6 fusion.106
  1516.6 3.2 fusion.53
  1519.8 14.4 fusion.54
  1535.1 41.5 %all-reduce.10.cloned.1.call-done = f32[512,4,32]{0,2,1:T(8,128)} async-done(((f32[512,4,32]{0,2,1:T(8,128)}), f32[512,4,32]{0,2,1:T(8,128)}) %all-reduce.10.cloned.1.call-update) | async-done | bytes 262160 | tf_op jit(solution)/shard_map/psum | solution.py:270
  1580.5 15.5 select_reduce_fusion
  1596.0 2.0 copy.116
  1598.0 1.8 convolution_convert_fusion
  1601.4 1.8 convolution_add_fusion
  1603.9 2.6 convolution_convert_fusion.1
  1606.8 66.3 %all-reduce.12.cloned.1.call-done = f32[512,1024]{1,0:T(8,128)} async-done(((f32[512,1024]{1,0:T(8,128)}), f32[512,1024]{1,0:T(8,128)}) %all-reduce.12.cloned.1.call-update) | async-done | bytes 2097168 | tf_op jit(solution)/shard_map/psum | solution.py:297
  1673.1 2.3 multiply_reduce_fusion.1
  1677.1 1.6 copy-done.1
  1684.7 2.5 fusion.109
  1687.3 2.8 fusion.112
  1690.1 2.7 fusion.111
  1692.9 2.8 fusion.37
  1695.8 3.1 fusion.56
  1699.0 4.8 fusion.110
  1706.0 1.9 reshape.458
  1707.9 4.0 fusion.65
  1713.7 26.4 sort
  1740.1 1.7 broadcast_clamp_fusion
  1743.0 1.7 reshape.459
  1744.7 23.5 bitcast_multiply_fusion
  1768.2 780.0 %scatter_custom_fusion.5 = f32[65536,256]{1,0:T(8,128)} fusion(s32[65536]{0:T(1024)} %get-tuple-element.102, f32[65536,256]{1,0:T(8,128)} %bitcast_multiply_fusion, s32[65536]{0:T(1024)} %broadcast_clamp_fusion, f32[]{:T(128)} %constant.223.clone.1), kind=kCustom, calls=%fused_computation.18 | custom fusion | flops 16777216 | bytes 67109376 | tf_op jit(solution)/shard_map/while/body/eval_jaxpr/scatter-add | solution.py:54
  2548.3 3.7 scatter_custom_fusion.2
  2552.0 4.7 all-to-all-start.1
  2556.7 1.6 convert_element_type.149
  2558.3 3.6 fusion.16
  2561.9 4.4 scatter_custom_fusion.4
  2566.3 34.1 %all-to-all-done.1 = f32[8,128,256]{2,1,0:T(8,128)S(1)} async-done(((f32[8,128,256]{2,1,0:T(8,128)}), f32[8,128,256]{2,1,0:T(8,128)S(1)}, u32[]{:S(2)}, u32[]{:S(2)}) %all-to-all-start.1) | async-done | bytes 1048608 | tf_op jit(solution)/shard_map/all_to_all | solution.py:345
  2600.4 3.6 all-to-all-start.3
  2605.3 2.2 gather_fusion.4
  2607.6 43.4 %all-reduce.2 = (f32[256]{0:T(256)S(1)}, f32[256]{0:T(256)S(1)}) all-reduce(f32[256]{0:T(256)S(1)} %dynamic_slice.30, f32[256]{0:T(256)S(1)} %dynamic_slice.31), channel_id=5, replica_groups=mesh['row'=8,'col'=4] {'row'}, use_global_device_ids=true, to_apply=%region_31.32.clone | all-reduce | flops 512 | bytes 4096
  2652.2 2.2 gather_fusion.7
  2654.5 567.4 %reduce-scatter.19.cloned.1.call-done = f32[8192,256]{1,0:T(8,128)} async-done(((f32[65536,256]{1,0:T(8,128)}), f32[8192,256]{1,0:T(8,128)}) %reduce-scatter.19.cloned.1.call-update) | async-done | bytes 8388624 | tf_op jit(solution)/shard_map/reduce_scatter | solution.py:343
  (233 shorter events, 49.0 us)
Async XLA Ops:
  29.8 96.8 %copy-start.39 = (s32[512]{0:T(512)}, s32[512]{0:T(512)S(1)}, u32[]{:S(2)}) copy-start(s32[512]{0:T(512)S(1)} %compare_select_fusion.2) | copy-start | bytes 6148
  29.8 28.1 copy-start.26
  33.3 25.3 copy-start.48
  33.3 25.4 copy-start.46
  33.3 33.5 %copy-start.29 = (f32[256,128]{1,0:T(8,128)S(1)}, f32[256,128]{1,0:T(8,128)}, u32[]{:S(2)}) copy-start(f32[256,128]{1,0:T(8,128)} %param.21) | copy-start | bytes 393220
  33.3 21.8 all-to-all-start
  39.8 43.5 %all-gather.16.cloned.1.call-start = ((), (), s32[]{:S(2)}) async-start(), calls=%async_computation.27 | async-start | bytes 1310720 | tf_op jit(solution)/shard_map/all_gather | solution.py:174
  43.7 37.3 %copy-start.41 = (s32[512]{0:T(512)}, s32[512]{0:T(512)S(1)}, u32[]{:S(2)}) copy-start(s32[512]{0:T(512)S(1)} %compare_select_fusion.3) | copy-start | bytes 6148
  57.8 52.9 %all-gather.10.cloned.1.call-start = ((), (), s32[]{:S(2)}) async-start(), calls=%async_computation.12 | async-start | bytes 1769472 | tf_op jit(solution)/shard_map/all_gather | solution.py:180
  58.5 135.6 %all-reduce.8.cloned.1.call-start = ((), (), s32[]{:S(2)}) async-start(), calls=%async_computation.13 | async-start | bytes 4194304 | tf_op jit(solution)/shard_map/psum | solution.py:210
  66.9 46.5 %copy-start.27 = (f32[4,1,256]{2,1,0:T(1,128)}, f32[4,1,256]{2,1,0:T(1,128)S(1)}, u32[]{:S(2)}) copy-start(f32[4,1,256]{2,1,0:T(1,128)S(1)} %convert_element_type.189) | copy-start | bytes 12292
  81.0 36.5 %copy-start.10 = (bf16[256,1024]{1,0:T(8,128)(2,1)}, bf16[256,1024]{1,0:T(8,128)(2,1)S(1)}, u32[]{:S(2)}) copy-start(bf16[256,1024]{1,0:T(8,128)(2,1)S(1)} %all_gather.40) | copy-start | bytes 1572868
  85.4 28.0 copy-start.33
  113.7 1.5 copy-start.16
  114.6 2.0 copy-start
  117.5 1.9 copy-start.21
  117.5 1.9 copy-start.25
  119.3 100.6 %all-gather.12.cloned.1.call-start = ((), (), s32[]{:S(2)}) async-start(), calls=%async_computation.14 | async-start | bytes 2359296 | tf_op jit(solution)/shard_map/all_gather | solution.py:181
  120.2 390.0 %all-gather.14.cloned.1.call-start = ((), (), s32[]{:S(2)}) async-start(), calls=%async_computation.15 | async-start | bytes 37748736 | tf_op jit(solution)/shard_map/all_gather | solution.py:187
  126.5 7.3 copy-start.47
  126.5 15.4 copy-start.30
  126.5 15.4 copy-start.31
  126.5 15.4 copy-start.32
  126.5 15.4 copy-start.14
  130.2 61.3 %all-to-all-start.2 = ((bf16[8,128,256]{2,1,0:T(8,128)(2,1)}), bf16[8,128,256]{2,1,0:T(8,128)(2,1)S(1)}, u32[]{:S(2)}, u32[]{:S(2)}) async-start(bf16[8,128,256]{2,1,0:T(8,128)(2,1)} %bitcast.30), calls=%async_computation.3 | async-start | bytes 1048576 | tf_op jit(solution)/shard_map/all_to_all | solution.py:165
  133.7 1382.8 %all-gather.18.cloned.1.call-start = ((), (), s32[]{:S(2)}) async-start(), calls=%async_computation.28 | async-start | bytes 1310720 | tf_op jit(solution)/shard_map/all_gather | solution.py:175
  142.0 33.7 %copy-start.42 = (s32[1024]{0:T(1024)}, s32[1024]{0:T(1024)S(1)}, u32[]{:S(2)}) copy-start(s32[1024]{0:T(1024)S(1)} %pad_clamp_fusion.1) | copy-start | bytes 12292
  144.7 49.5 %copy-start.2 = (bf16[512,1024]{1,0:T(8,128)(2,1)S(1)}, bf16[512,1024]{1,0:T(8,128)(2,1)}, u32[]{:S(2)}) copy-start(bf16[512,1024]{1,0:T(8,128)(2,1)} %all-gather.16.cloned.1.call-done) | copy-start | bytes 3145732
  194.1 1382.6 %all-reduce.10.cloned.1.call-start = ((), (), s32[]{:S(2)}) async-start(), calls=%async_computation.17 | async-start | bytes 524288 | tf_op jit(solution)/shard_map/psum | solution.py:270
  196.1 1.8 copy-start.7
  219.9 4.2 copy-start.9
  224.2 1.3 copy-start.6
  251.8 1251.1 %copy-start.23 = (bf16[512,4,32]{0,2,1:T(8,128)(2,1)}, bf16[512,4,32]{0,2,1:T(8,128)(2,1)S(1)}, u32[]{:S(2)}) copy-start(bf16[512,4,32]{0,2,1:T(8,128)(2,1)S(1)} %get-tuple-element.150) | copy-start | bytes 393220
  1535.1 138.0 %all-reduce.12.cloned.1.call-start = ((), (), s32[]{:S(2)}) async-start(), calls=%async_computation.18 | async-start | bytes 4194304 | tf_op jit(solution)/shard_map/psum | solution.py:297
  1598.0 1.9 copy-start.44
  1599.9 1.4 copy-start.20
  1599.9 1.4 copy-start.8
  1599.9 1.4 copy-start.19
  1603.2 945.1 %reduce-scatter.9.cloned.1.call-start = ((), (), s32[]{:S(2)}) async-start(), calls=%async_computation.16 | async-start | bytes 1310720 | tf_op jit(solution)/shard_map/reduce_scatter | solution.py:250
  1606.5 68.8 %copy-start.38 = (f32[512]{0:T(512)S(1)}, f32[512]{0:T(512)}, u32[]{:S(2)}) copy-start(f32[512]{0:T(512)} %get-tuple-element.136) | copy-start | bytes 6148
  1606.5 951.8 %all-reduce.14.cloned.1.call-start = ((), (), s32[]{:S(2)}) async-start(), calls=%async_computation.19 | async-start | bytes 4194304 | tf_op jit(solution)/shard_map/psum | solution.py:319
  1673.0 2.3 copy-start.5
  1673.1 2.5 copy-start.12
  1675.5 1.0 copy-start.11
  1675.5 3.1 copy-start.1
  1676.6 3.2 copy-start.3
  1676.6 2.3 copy-start.17
  1683.0 1.7 copy-start.45
  1687.2 967.2 %reduce-scatter.23.cloned.1.call-start = ((), (), s32[]{:S(2)}) async-start(), calls=%async_computation.26 | async-start | bytes 1179648 | tf_op jit(solution)/shard_map/reduce_scatter | solution.py:330
  1690.1 964.4 %reduce-scatter.21.cloned.1.call-start = ((), (), s32[]{:S(2)}) async-start(), calls=%async_computation.25 | async-start | bytes 1179648 | tf_op jit(solution)/shard_map/reduce_scatter | solution.py:328
  1692.9 3.0 copy-start.22
  1692.9 961.6 %reduce-scatter.17.cloned.1.call-start = ((), (), s32[]{:S(2)}) async-start(), calls=%async_computation.23 | async-start | bytes 1179648 | tf_op jit(solution)/shard_map/reduce_scatter | solution.py:331
  1695.8 958.7 %reduce-scatter.13.cloned.1.call-start = ((), (), s32[]{:S(2)}) async-start(), calls=%async_computation.21 | async-start | bytes 1179648 | tf_op jit(solution)/shard_map/reduce_scatter | solution.py:329
  1698.9 955.5 %reduce-scatter.15.cloned.1.call-start = ((), (), s32[]{:S(2)}) async-start(), calls=%async_computation.22 | async-start | bytes 4718592 | tf_op jit(solution)/shard_map/reduce_scatter | solution.py:327
  1703.8 4.1 copy-start.28
  1703.8 4.1 copy-start.34
  1703.8 950.7 %reduce-scatter.11.cloned.1.call-start = ((), (), s32[]{:S(2)}) async-start(), calls=%async_computation.20 | async-start | bytes 3538944 | tf_op jit(solution)/shard_map/reduce_scatter | solution.py:326
  1712.0 29.8 copy-start.24
  1712.0 1509.9 %reduce-scatter.19.cloned.1.call-start = ((), (), s32[]{:S(2)}) async-start(), calls=%async_computation.24 | async-start | bytes 75497472 | tf_op jit(solution)/shard_map/reduce_scatter | solution.py:343
  2552.0 48.4 %all-to-all-start.1 = ((f32[8,128,256]{2,1,0:T(8,128)}), f32[8,128,256]{2,1,0:T(8,128)S(1)}, u32[]{:S(2)}, u32[]{:S(2)}) async-start(f32[8,128,256]{2,1,0:T(8,128)} %bitcast.183), calls=%async_computation.2 | async-start | bytes 2097152 | tf_op jit(solution)/shard_map/all_to_all | solution.py:345
  2558.3 3.6 copy-start.37
  2561.9 42.1 %copy-start.49 = (u32[32]{0:T(128)S(1)}, u32[32]{0:T(128)}, u32[]{:S(2)}) copy-start(u32[32]{0:T(128)} %constant.256) | copy-start | bytes 388
  2561.9 43.3 %copy-start.40 = (s32[512]{0:T(512)S(1)}, s32[512]{0:T(512)}, u32[]{:S(2)}) copy-start(s32[512]{0:T(512)} %copy-done.39) | copy-start | bytes 6148
  2600.4 51.8 %all-to-all-start.3 = ((f32[8,128,256]{2,1,0:T(8,128)}), f32[8,128,256]{2,1,0:T(8,128)S(1)}, u32[]{:S(2)}, u32[]{:S(2)}) async-start(f32[8,128,256]{2,1,0:T(8,128)} %bitcast.46), calls=%async_computation.4 | async-start | bytes 2097152 | tf_op jit(solution)/shard_map/all_to_all | solution.py:352
  (7 other events, 6.4 us)
Sparse Core Ops, SparseCore 0:
  57.9 25.3 all-gather.15
  85.5 25.0 all-gather.9
  119.5 69.1 all-reduce.7
  190.8 29.1 all-gather.11
  222.0 288.1 all-gather.13
  512.0 24.6 all-gather.17
  1535.2 41.4 all-reduce.9
  1603.4 69.6 all-reduce.11
  1676.2 27.8 reduce-scatter.8
  1707.0 69.6 all-reduce.13
  1779.7 32.3 reduce-scatter.22
  1814.9 30.6 reduce-scatter.20
  1848.5 30.6 reduce-scatter.16
  1882.0 30.5 reduce-scatter.12
  1915.4 48.2 reduce-scatter.14
  1966.5 38.4 reduce-scatter.10
  2548.4 673.4 reduce-scatter.18
where the time goes:
time: 3260 us; the launch traced here: 3230 us
  local copies, waits for them, and re-layouts  1050 us (32%)
  waiting for transfers between devices  1030 us (32%)
  other arithmetic  903 us (28%)
  blocking collectives  132 us (4%)
  matrix products  76.1 us (2%)
    gather x1, local copies, waits for them, and re-layouts, read_memory(): table_rows[picks_flat]  993 us
    scatter-add x3, other arithmetic, add_block(): total.at[target.reshape(-1)].add(update.reshape(-1, width), mode='drop')  808 us
    reduce_scatter x1, waiting for transfers between devices, per_device(): lax.psum_scatter(table_total, 'row', scatter_dimension=0, tiled=True)  567 us
    all_gather x1, waiting for transfers between devices, per_device(): lax.all_gather(value_table.astype(jnp.bfloat16), 'row', axis=0, tiled=True)  258 us
    psum x1, waiting for transfers between devices, per_device(): grad_hidden_two = lax.psum(hidden_two_part, 'col')  66.3 us
  transfers between devices with their start and end apart: 21, of which 9 were waited for; matrix products, arithmetic and copies ran while one was open for 60% of the time, Pallas kernels for 0%

commit v1 on v0

--- a/solution.py
+++ b/solution.py
@@ -1,6 +1,10 @@
+import functools
+
 import jax
 import jax.numpy as jnp
 from jax import lax
+from jax.experimental import pallas as pl
+from jax.experimental.pallas import tpu as pltpu
 from jax.sharding import PartitionSpec as P
 
 D = 1024
@@ -39,23 +43,134 @@
     return (seq_ids[:, None] == seq_ids[None, :]) & (query_pos[:, None] >= places[None, :])
 
 
-def scatter_picks(accum, base_row, weights_low, grads_low, picks):
-    span = accum.shape[0]
-    width = accum.shape[1]
-    rows = picks.shape[0]
-
-    def add_block(total, start_blk):
-        pick_blk = picks - base_row
-        inside = (pick_blk >= 0) & (pick_blk < span)
-        target = jnp.where(inside, pick_blk, span)
-        weight_blk = weights_low.astype(jnp.float32)
-        grad_blk = grads_low.astype(jnp.float32)
-        update = weight_blk[:, :, None] * grad_blk[:, None, :]
-        return (total.at[target.reshape(-1)].add(update.reshape(-1, width), mode="drop"), None)
-
-    starts = jnp.arange(rows // rows, dtype=jnp.int32) * rows
-    total, unused = lax.scan(add_block, accum, starts)
-    return total
+NT_DIMS = (((1,), (1,)), ((), ()))
+LANES = 128
+
+
+def memory_kernel(
+    groups, tok_block, iters, hi_ref, lo_ref, w_ref, dm_ref, table_ref, mem_ref, dw_ref, gt_ref, dense, gacc
+):
+    f32, low = jnp.float32, jnp.bfloat16
+    spans = groups * NK // LANES
+    pitch = spans + 8
+    per_tok = tok_block // iters
+    per_span = spans // iters
+    step = pl.program_id(0)
+
+    @pl.when(step == 0)
+    def _():
+        gacc[...] = jnp.zeros_like(gacc)
+
+    places_lo = lax.broadcasted_iota(jnp.int32, (LANES, LANES), 0).astype(f32).astype(low)
+    places_hi = lax.broadcasted_iota(jnp.int32, (spans, LANES), 0).astype(f32).astype(low)
+    ones = jnp.ones((LANES, LANES), low)
+    zeros = jnp.zeros((LANES, LANES), low)
+    blank = jnp.zeros((spans, LANES), low)
+    grads = dm_ref[...]
+    grads_t = grads.T
+    mem_ref[...] = jnp.zeros_like(mem_ref)
+    dw_ref[...] = jnp.zeros_like(dw_ref)
+    lo_int = lo_ref[...].astype(jnp.int32)
+    hi_all = hi_ref[...]
+
+    def token_pair(first):
+        rights, lefts = [], []
+        for token in (first, first + 1):
+            lo_row = jnp.broadcast_to(lo_ref[pl.ds(token, 1), :], (LANES, LANES)).astype(low)
+            hi_row = jnp.broadcast_to(hi_ref[pl.ds(token, 1), :], (spans, LANES)).astype(low)
+            w_row = jnp.broadcast_to(w_ref[pl.ds(token, 1), :], (spans, LANES)).astype(low)
+            rights.append(jnp.where(lo_row == places_lo, ones, zeros))
+            lefts.append(jnp.where(hi_row == places_hi, w_row, blank))
+        right = jnp.concatenate(rights, axis=1)
+        left = jnp.concatenate(
+            [
+                jnp.concatenate([lefts[0], blank], axis=1),
+                jnp.concatenate([blank, lefts[1]], axis=1),
+            ],
+            axis=0,
+        )
+        both = lax.dot_general(left, right, NT_DIMS, preferred_element_type=f32)
+        for j in range(2):
+            dense[pl.ds(pl.multiple_of((first + j) * pitch, 8), spans), :] = both[
+                j * spans : (j + 1) * spans
+            ]
+
+    def build(it, _):
+        rows = pl.ds(pl.multiple_of(it * per_span * LANES, LANES), per_span * LANES)
+        products = lax.dot_general(
+            grads, table_ref[rows, :], NT_DIMS, preferred_element_type=f32
+        )
+        found = dw_ref[...]
+        pairs = per_tok // 2 // per_span
+        for j in range(per_span):
+            picked = jnp.take_along_axis(
+                products[:, LANES * j : LANES * (j + 1)], lo_int, axis=1
+            )
+            found = jnp.where(hi_all == (it * per_span + j).astype(f32), picked, found)
+            for u in range(pairs):
+                token_pair(it * per_tok + (j * pairs + u) * 2)
+        dw_ref[...] = found
+        return 0
+
+    lax.fori_loop(0, iters, build, 0)
+
+    def multiply(it, _):
+        rows = pl.ds(pl.multiple_of(it * per_span * LANES, LANES), per_span * LANES)
+        weights = jnp.concatenate(
+            [
+                dense[pl.ds(it * per_span + j, tok_block, stride=pitch), :].astype(low)
+                for j in range(per_span)
+            ],
+            axis=1,
+        )
+        mem_ref[...] += jnp.dot(weights, table_ref[rows, :], preferred_element_type=f32)
+        gacc[:, rows] += jnp.dot(grads_t, weights, preferred_element_type=f32)
+        return 0
+
+    lax.fori_loop(0, iters, multiply, 0)
+
+    @pl.when(step == pl.num_programs(0) - 1)
+    def _():
+        def turn(i, _):
+            rows = pl.ds(pl.multiple_of(i * NK, NK), NK)
+            gt_ref[rows, :] = gacc[:, rows].T
+            return 0
+
+        lax.fori_loop(0, groups, turn, 0)
+
+
+def memory_call(hi, lo, weights, grads, table):
+    tokens, picks = hi.shape
+    rows, width = table.shape
+    groups = rows // NK
+    tok_block = 512
+    spec = lambda n: pl.BlockSpec((tok_block, n), lambda i: (i, 0))
+    return pl.pallas_call(
+        functools.partial(memory_kernel, groups, tok_block, 4),
+        grid=(tokens // tok_block,),
+        in_specs=[
+            spec(picks),
+            spec(picks),
+            spec(picks),
+            spec(width),
+            pl.BlockSpec((rows, width), lambda i: (0, 0)),
+        ],
+        out_specs=[
+            spec(width),
+            spec(picks),
+            pl.BlockSpec((rows, width), lambda i: (0, 0), pipeline_mode=pl.Buffered(1)),
+        ],
+        out_shape=[
+            jax.ShapeDtypeStruct((tokens, width), jnp.float32),
+            jax.ShapeDtypeStruct((tokens, picks), jnp.float32),
+            jax.ShapeDtypeStruct((rows, width), jnp.float32),
+        ],
+        scratch_shapes=[
+            pltpu.VMEM((tok_block * (rows // LANES + 8), LANES), jnp.float32),
+            pltpu.VMEM((width, rows), jnp.float32),
+        ],
+        compiler_params=pltpu.CompilerParams(vmem_limit_bytes=62 * 2**20),
+    )(hi, lo, weights, grads, table)
 
 
 def attention_forward(queries, key_rows, value_rows, seq_ids, score_scale):
@@ -184,7 +299,10 @@
         lax.all_gather(w_mem_out.astype(jnp.bfloat16), "row", axis=1, tiled=True),
         lax.all_gather(sub_keys.astype(jnp.bfloat16), "row", axis=1, tiled=True),
     )
-    table_rows = lax.all_gather(value_table.astype(jnp.bfloat16), "row", axis=0, tiled=True)
+    own_rows = value_table.shape[0]
+    picks_all = lax.all_gather(value_picks.reshape(tok_rows, MH * PICKS), "row", axis=0, tiled=True)
+    picks_hi = (picks_all // LANES - row_index * (own_rows // LANES)).astype(jnp.float32)
+    picks_lo = (picks_all % LANES).astype(jnp.float32)
     heads_here = col_width // HD
     halves_here = query_weight.shape[1] // QD
     score_scale = HD ** (-0.5)
@@ -232,42 +350,37 @@
     score = jnp.sum(gathered.reshape(tok_rows, MH, 2, PICKS), axis=2)
     pick_weights = jax.nn.softmax(score, axis=-1).reshape(tok_rows, MH * PICKS)
     pick_weights_low = pick_weights.astype(jnp.bfloat16)
-    picks_flat = value_picks.reshape(tok_rows, MH * PICKS)
-
-    def read_memory(start_row):
-        return jnp.einsum(
-            "tp,tpd->td",
-            pick_weights_low,
-            table_rows[picks_flat],
-            preferred_element_type=jnp.float32,
-        )
-
-    memory = lax.map(read_memory, starts).reshape(tok_rows, col_width)
     gate = jnp.dot(hidden_two, gate_weight, preferred_element_type=jnp.float32)
     sigmoid_gate = jax.nn.sigmoid(gate)
+    grad_mixed_two = jnp.einsum(
+        "tD,cD->tc", full_cot, memout_weight, preferred_element_type=jnp.float32
+    )
+    grad_memory = (grad_mixed_two * gate * sigmoid_gate).astype(jnp.bfloat16)
+    sent = lax.all_gather(
+        jnp.concatenate([pick_weights_low, grad_memory], axis=1), "row", axis=0, tiled=True
+    )
+    mem_part, dw_part, grad_table = memory_call(
+        picks_hi,
+        picks_lo,
+        sent[:, : MH * PICKS].astype(jnp.float32),
+        sent[:, MH * PICKS :],
+        value_table.astype(jnp.bfloat16),
+    )
+    memory = lax.psum_scatter(mem_part, "row", scatter_dimension=0, tiled=True)
+    grad_weight_pick = lax.psum(
+        lax.psum_scatter(dw_part, "row", scatter_dimension=0, tiled=True), "col"
+    )
     mixed_two = (memory * gate * sigmoid_gate).astype(jnp.bfloat16)
     memout_part = jnp.dot(mixed_two, memout_weight, preferred_element_type=jnp.float32)
     memory_out = lax.psum_scatter(
         memout_part.astype(jnp.bfloat16), "col", scatter_dimension=1, tiled=True
     ).astype(jnp.float32)
     result_block = lax.dynamic_slice_in_dim(resid, col_index * col_width, col_width, 1) + memory_out
-    grad_mixed_two = jnp.einsum(
-        "tD,cD->tc", full_cot, memout_weight, preferred_element_type=jnp.float32
-    )
     grad_memout_w = jnp.einsum("tc,tD->cD", mixed_two, full_cot, preferred_element_type=jnp.float32)
-    grad_memory = (grad_mixed_two * gate * sigmoid_gate).astype(jnp.bfloat16)
     grad_gate = (
         grad_mixed_two * memory * sigmoid_gate * (1.0 + gate * (1.0 - sigmoid_gate))
     ).astype(jnp.bfloat16)
     grad_gate_w = jnp.einsum("tD,tc->Dc", hidden_two, grad_gate, preferred_element_type=jnp.float32)
-    table_back = lax.all_gather(value_table.astype(jnp.bfloat16), "row", axis=0, tiled=True)
-
-    def pick_grad(start_row):
-        return jnp.einsum(
-            "td,tpd->tp", grad_memory, table_back[picks_flat], preferred_element_type=jnp.float32
-        )
-
-    grad_weight_pick = lax.psum(lax.map(pick_grad, starts).reshape(tok_rows, MH * PICKS), "col")
     weights_grouped = pick_weights.reshape(tok_rows, MH, PICKS)
     pick_grad_grouped = grad_weight_pick.reshape(tok_rows, MH, PICKS)
     grad_score = weights_grouped * (
@@ -332,15 +445,6 @@
         lax.psum_scatter(gain_one_block, "row", scatter_dimension=0, tiled=True),
         lax.psum_scatter(gain_two_block, "row", scatter_dimension=0, tiled=True),
     )
-    own_rows = value_table.shape[0]
-    table_total = scatter_picks(
-        jnp.zeros((own_rows * row_count, col_width), jnp.float32),
-        0,
-        pick_weights_low,
-        grad_memory,
-        picks_flat,
-    )
-    grad_table = lax.psum_scatter(table_total, "row", scatter_dimension=0, tiled=True)
     got_result, got_grad = (
         lax.all_to_all(
             pack_rows(result_block, recv_pos, slot_count),

time: 3260 us -> 1040 us (0.32)
  local copies, waits for them, and re-layouts: 1050 us -> 55.9 us
  other arithmetic: 903 us -> 75.9 us
  waiting for transfers between devices: 1030 us -> 523 us
  Pallas kernels: 0 us -> 152 us
    gather x1 -> x0, local copies, waits for them, and re-layouts: 993 us -> none  [read_memory(): table_rows[picks_flat]]
    scatter-add x3 -> x0, other arithmetic: 808 us -> none  [add_block(): total.at[target.reshape(-1)].add(update.reshape(-1, width), mode='drop')]
    reduce_scatter x1 -> x2, waiting for transfers between devices: 567 us -> 64.4 us  [the longest x1 34.7 us: per_device(): lax.psum_scatter(dw_part, 'row', scatter_dimension=0, tiled=True)]
    all_gather x1 -> x2, waiting for transfers between devices: 258 us -> 51.6 us  [the longest x1 34.5 us: per_device(): lax.all_gather(jnp.concatenate([pick_weights_low, grad_memory], axis=1),...]
    pallas_call x0 -> x1, Pallas kernels: none -> 152 us  [memory_call(): pl.pallas_call(functools.partial(memory_kernel, groups, tok_block, 4), gr...]
    psum x1, waiting for transfers between devices: 0.01 us -> 58.6 us  [per_device(): grad_hidden_one = lax.psum(hidden_one_part, 'col')]
    reduce_scatter x1, waiting for transfers between devices: 0.02 us -> 51 us  [per_device(): lax.psum_scatter(grad_query_w, 'row', scatter_dimension=0, tiled=True)]
    reduce_scatter x1, waiting for transfers between devices: 0.02 us -> 41.5 us  [per_device(): lax.psum_scatter(grad_qkv_w, 'row', scatter_dimension=0, tiled=True)]
  transfers between devices with their start and end apart: 21 -> 22, of which waited for: 9 -> 16; matrix products, arithmetic and copies ran while one was open for 60% -> 12% of each run, Pallas kernels for 0% -> 0%
where the time goes in v1:
time: 1040 us; the launch traced here: 1030 us
  waiting for transfers between devices  523 us (50%)
  Pallas kernels  152 us (15%)
  blocking collectives  143 us (14%)
  other arithmetic  75.9 us (7%)
  local copies, waits for them, and re-layouts  55.9 us (5%)
  matrix products  50.2 us (5%)
  starting transfers between devices  17.6 us (2%)
  between operations  15.8 us (2%)
    pallas_call x1, Pallas kernels, memory_call(): pl.pallas_call(functools.partial(memory_kernel, groups, tok_block, 4), gr...  152 us
    psum x1, waiting for transfers between devices, per_device(): grad_hidden_two = lax.psum(hidden_two_part, 'col')  65 us
    psum x1, waiting for transfers between devices, per_device(): grad_hidden_one = lax.psum(hidden_one_part, 'col')  58.6 us
    reduce_scatter x1, waiting for transfers between devices, per_device(): lax.psum_scatter(grad_query_w, 'row', scatter_dimension=0, tiled=True)  51 us
    psum x1, waiting for transfers between devices, per_device(): lax.psum(lax.psum_scatter(dw_part, 'row', scatter_dimension=0, tiled=True...  42.8 us
    reduce_scatter x1, waiting for transfers between devices, per_device(): lax.psum_scatter(grad_qkv_w, 'row', scatter_dimension=0, tiled=True)  41.5 us
    reduce_scatter x1, waiting for transfers between devices, per_device(): lax.psum_scatter(dw_part, 'row', scatter_dimension=0, tiled=True)  34.7 us
    all_gather x1, waiting for transfers between devices, per_device(): lax.all_gather(jnp.concatenate([pick_weights_low, grad_memory], axis=1),...  34.5 us
  transfers between devices with their start and end apart: 22, of which 16 were waited for; matrix products, arithmetic and copies ran while one was open for 12% of the time, Pallas kernels for 0%

profile of v1, /device:TPU:0, one launch (start us, length us, event | category | flops | bytes accessed | tf_op | source)
XLA Modules:
  0.0 1033.1 jit_solution(15587448938871416703)
XLA Ops:
  10.9 15.5 %scatter_custom_fusion = s32[4096]{0:T(1024)S(1)} fusion(s32[4096]{0:T(1024)S(1)} %add_select_fusion.5, s32[4096]{0:T(1024)S(1)} %iota.46, s32[]{:T(128)} %constant.219.clone.1), kind=kCustom, calls=%fused_computation.159 | custom fusion | bytes 16388 | tf_op jit(solution)/shard_map/scatter | solution.py:272
  26.5 3.1 gather_fusion
  29.8 3.6 scatter_custom_fusion.1
  33.3 6.5 all-to-all-start
  43.7 11.5 %all-to-all-done = bf16[8,128,256]{2,1,0:T(8,128)(2,1)S(1)} async-done(((bf16[8,128,256]{2,1,0:T(8,128)(2,1)}), bf16[8,128,256]{2,1,0:T(8,128)(2,1)S(1)}, u32[]{:S(2)}, u32[]{:S(2)}) %all-to-all-start) | async-done | bytes 524320 | tf_op jit(solution)/shard_map/all_to_all | solution.py:277
  55.2 2.6 gather_fusion.1
  58.6 8.1 all-gather.2
  67.0 14.0 %all_gather.42 = bf16[256,1024]{1,0:T(8,128)(2,1)S(1)} all-gather(bf16[256,128]{1,0:T(8,128)(2,1)S(1)} %convert_element_type.148), channel_id=1, replica_groups=mesh['row'=8,'col'=4] {'row'}, dimensions={1}, use_global_device_ids=true | all-gather | bytes 589824 | tf_op jit(solution)/shard_map/all_gather | solution.py:298
  81.2 2.1 all-gather.19.cloned.1.call-done
  84.8 25.8 %all-gather.11.cloned.1.call-done = bf16[1024,768]{1,0:T(8,128)(2,1)} async-done(((bf16[128,768]{1,0:T(8,128)(2,1)}), bf16[1024,768]{1,0:T(8,128)(2,1)}) %all-gather.11.cloned.1.call-update) | async-done | bytes 1572880 | tf_op jit(solution)/shard_map/all_gather | solution.py:295
  110.6 2.8 convolution_convert_fusion.3
  117.4 1.8 fusion.96
  120.6 2.9 scatter_custom_fusion.2
  123.5 18.5 %all_to_all.48 = bf16[8,128,256]{2,1,0:T(8,128)(2,1)S(1)} all-to-all(bf16[8,128,256]{2,1,0:T(8,128)(2,1)S(1)} %bitcast.160), channel_id=1, replica_groups=mesh['row'=8,'col'=4] {'row'}, dimensions={0} | all-to-all | bytes 1048576 | tf_op jit(solution)/shard_map/all_to_all | solution.py:280
  142.0 2.6 gather_fusion.3
  145.6 8.0 all-gather.3
  153.7 15.9 %all_gather.50 = bf16[1024,256]{1,0:T(8,128)(2,1)} all-gather(bf16[128,256]{1,0:T(8,128)(2,1)S(1)} %convert_element_type.160), channel_id=1, replica_groups=mesh['row'=8,'col'=4] {'row'}, dimensions={0}, use_global_device_ids=true | all-gather | bytes 589824 | tf_op jit(solution)/shard_map/all_gather | solution.py:297
  169.6 14.7 %all_gather.49 = bf16[256,1024]{1,0:T(8,128)(2,1)} all-gather(bf16[256,128]{1,0:T(8,128)(2,1)S(1)} %convert_element_type.159), channel_id=1, replica_groups=mesh['row'=8,'col'=4] {'row'}, dimensions={1}, use_global_device_ids=true | all-gather | bytes 589824 | tf_op jit(solution)/shard_map/all_gather | solution.py:299
  184.3 15.8 %all_gather.46 = bf16[2,256,512]{2,1,0:T(8,128)(2,1)} all-gather(bf16[2,32,512]{2,1,0:T(8,128)(2,1)S(1)} %convert_element_type.156), channel_id=1, replica_groups=mesh['row'=8,'col'=4] {'row'}, dimensions={1}, use_global_device_ids=true | all-gather | bytes 589824 | tf_op jit(solution)/shard_map/all_gather | solution.py:300
  201.2 1.9 multiply_reduce_fusion.3
  204.7 15.1 %all-gather.15.cloned.1.call-done = bf16[1024,1024]{1,0:T(8,128)(2,1)} async-done(((bf16[128,1024]{1,0:T(8,128)(2,1)}), bf16[1024,1024]{1,0:T(8,128)(2,1)}) %all-gather.15.cloned.1.call-update) | async-done | bytes 2097168 | tf_op jit(solution)/shard_map/all_gather | solution.py:296
  219.8 2.9 convolution_convert_fusion.2
  225.0 11.5 %select_reduce_fusion.1 = f32[512,2,32]{2,1,0:T(2,128)} fusion(f32[512,2,256]{2,1,0:T(2,128)S(1)} %copy.107, s32[512,2,32]{2,1,0:T(2,128)S(1)} %copy.105), kind=kLoop, calls=%fused_computation.16 | loop fusion | flops 25133056 | bytes 1310720 | tf_op jit(solution)/shard_map/while/body/eval_jaxpr/reduce_sum | solution.py:346
  237.7 14.6 %all_gather.47 = f32[512,256]{0,1:T(8,128)} all-gather(f32[512,64]{0,1:T(8,128)S(1)} %bitcast.166), channel_id=1, replica_groups=mesh['row'=8,'col'=4] {'col'}, dimensions={1}, use_global_device_ids=true | all-gather | bytes 655360 | tf_op jit(solution)/shard_map/all_gather | solution.py:349
  253.6 2.3 fusion.97
  255.9 2.8 multiply_convert_fusion.4
  259.7 6.1 convert_element_type.163.table_ref
  265.8 17.0 %all-gather.13.cloned.1.call-done = s32[4096,128]{1,0:T(8,128)} async-done(((s32[512,128]{1,0:T(8,128)}), s32[4096,128]{1,0:T(8,128)}) %all-gather.13.cloned.1.call-update) | async-done | bytes 2097168 | tf_op jit(solution)/shard_map/all_gather | solution.py:303
  282.8 5.6 fusion.13
  288.4 34.5 %all-gather.17.cloned.1.call-done = bf16[4096,384]{1,0:T(8,128)(2,1)} async-done(((bf16[512,384]{1,0:T(8,128)(2,1)}), bf16[4096,384]{1,0:T(8,128)(2,1)}) %all-gather.17.cloned.1.call-update) | async-done | bytes 3145744 | tf_op jit(solution)/shard_map/all_gather | solution.py:359
  322.9 2.9 slice_convert_fusion.w_ref
  327.3 152.2 %shard_map.221 = (f32[4096,256]{1,0:T(8,128)}, f32[4096,128]{1,0:T(8,128)}, f32[8192,256]{1,0:T(8,128)}) custom-call(f32[4096,128]{1,0:T(8,128)} %get-tuple-element.108.hi_ref, f32[4096,128]{1,0:T(8,128)} %get-tuple-element.97.lo_ref, f32[4096,128]{1,0:T(8,128)} %slice_convert_fusion.w_ref, bf16[4096,256]{1,0:T(8,128)(2,1)} %slice.56.dm_ref, ...), custom_call_target="tpu_custom_call" | custom-call | tf_op jit(solution)/shard_map/pallas_call | solution.py:148
  479.6 34.7 %reduce-scatter.14.cloned.1.call-done = f32[512,128]{1,0:T(8,128)} async-done(((f32[4096,128]{1,0:T(8,128)}), f32[512,128]{1,0:T(8,128)}) %reduce-scatter.14.cloned.1.call-update) | async-done | bytes 262160 | tf_op jit(solution)/shard_map/reduce_scatter | solution.py:371
  514.3 1.8 copy.114
  516.7 42.8 %all-reduce.10.cloned.1.call-done = f32[512,4,32]{0,2,1:T(8,128)} async-done(((f32[512,4,32]{0,2,1:T(8,128)}), f32[512,4,32]{0,2,1:T(8,128)}) %all-reduce.10.cloned.1.call-update) | async-done | bytes 262160 | tf_op jit(solution)/shard_map/psum | solution.py:370
  561.5 14.3 %select_reduce_fusion = bf16[512,2,256]{2,1,0:T(2,128)(2,1)} fusion(f32[512,2,32]{2,1,0:T(2,128)S(1)} %copy.115, s32[512,2,32]{2,1,0:T(2,128)S(1)} %copy.105), kind=kLoop, calls=%fused_computation.15 | loop fusion | flops 24903680 | bytes 786432 | tf_op jit(solution)/shard_map/while/body/eval_jaxpr/reduce_sum | solution.py:393
  579.3 2.7 fusion.98
  582.0 29.7 %reduce-scatter.10.cloned.1.call-done = f32[512,256]{1,0:T(8,128)} async-done(((f32[4096,256]{1,0:T(8,128)}), f32[512,256]{1,0:T(8,128)}) %reduce-scatter.10.cloned.1.call-update) | async-done | bytes 524304 | tf_op jit(solution)/shard_map/reduce_scatter | solution.py:369
  613.0 3.5 convolution_add_fusion
  616.8 2.6 convolution_convert_fusion.1
  619.5 65.0 %all-reduce.12.cloned.1.call-done = f32[512,1024]{1,0:T(8,128)} async-done(((f32[512,1024]{1,0:T(8,128)}), f32[512,1024]{1,0:T(8,128)}) %all-reduce.12.cloned.1.call-update) | async-done | bytes 2097168 | tf_op jit(solution)/shard_map/psum | solution.py:410
  684.5 2.3 multiply_reduce_fusion.1
  688.5 1.6 copy-done.1
  696.2 2.5 fusion.99
  698.7 2.9 fusion.36
  701.7 2.8 fusion.101
  704.5 2.7 fusion.102
  707.3 3.1 fusion.48
  710.5 4.8 fusion.100
  715.6 4.0 fusion.57
  719.7 3.7 scatter_custom_fusion.3
  723.4 4.6 all-to-all-start.2
  729.5 58.6 %all-reduce.14.cloned.1.call-done = f32[512,1024]{1,0:T(8,128)} async-done(((f32[512,1024]{1,0:T(8,128)}), f32[512,1024]{1,0:T(8,128)}) %all-reduce.14.cloned.1.call-update) | async-done | bytes 2097168 | tf_op jit(solution)/shard_map/psum | solution.py:432
  788.1 3.7 fusion.10
  791.8 4.3 scatter_custom_fusion.4
  796.1 4.6 all-to-all-start.3
  802.0 2.2 gather_fusion.4
  804.3 33.4 %all-reduce.2 = (f32[256]{0:T(256)S(1)}, f32[256]{0:T(256)S(1)}) all-reduce(f32[256]{0:T(256)S(1)} %dynamic_slice.30, f32[256]{0:T(256)S(1)} %dynamic_slice.31), channel_id=7, replica_groups=mesh['row'=8,'col'=4] {'row'}, use_global_device_ids=true, to_apply=%region_33.34.clone | all-reduce | flops 512 | bytes 4096
  839.0 2.2 gather_fusion.6
  841.2 25.4 %reduce-scatter.24.cloned.1.call-done = f32[128,256]{1,0:T(8,128)} async-done(((f32[1024,256]{1,0:T(8,128)}), f32[128,256]{1,0:T(8,128)}) %reduce-scatter.24.cloned.1.call-update) | async-done | bytes 131088 | tf_op jit(solution)/shard_map/reduce_scatter | solution.py:441
  866.6 33.6 %reduce-scatter.26.cloned.1.call-done = f32[256,128]{1,0:T(8,128)} async-done(((f32[256,1024]{1,0:T(8,128)}), f32[256,128]{1,0:T(8,128)}) %reduce-scatter.26.cloned.1.call-update) | async-done | bytes 131088 | tf_op jit(solution)/shard_map/reduce_scatter | solution.py:443
  900.2 33.5 %reduce-scatter.18.cloned.1.call-done = f32[256,128]{1,0:T(8,128)} async-done(((f32[256,1024]{1,0:T(8,128)}), f32[256,128]{1,0:T(8,128)}) %reduce-scatter.18.cloned.1.call-update) | async-done | bytes 131088 | tf_op jit(solution)/shard_map/reduce_scatter | solution.py:442
  933.6 51.0 %reduce-scatter.20.cloned.1.call-done = f32[128,1024]{1,0:T(8,128)} async-done(((f32[1024,1024]{1,0:T(8,128)}), f32[128,1024]{1,0:T(8,128)}) %reduce-scatter.20.cloned.1.call-update) | async-done | bytes 524304 | tf_op jit(solution)/shard_map/reduce_scatter | solution.py:440
  984.7 41.5 %reduce-scatter.16.cloned.1.call-done = f32[128,768]{1,0:T(8,128)} async-done(((f32[1024,768]{1,0:T(8,128)}), f32[128,768]{1,0:T(8,128)}) %reduce-scatter.16.cloned.1.call-update) | async-done | bytes 393232 | tf_op jit(solution)/shard_map/reduce_scatter | solution.py:439
  (205 shorter events, 46.4 us)
Async XLA Ops:
  29.8 28.0 %copy-start.27 = (f32[128,768]{1,0:T(8,128)S(1)}, f32[128,768]{1,0:T(8,128)}, u32[]{:S(2)}) copy-start(f32[128,768]{1,0:T(8,128)} %param.20) | copy-start | bytes 1179652
  33.3 25.3 %copy-start.34 = (f32[256]{0:T(256)S(1)}, f32[256]{0:T(256)}, u32[]{:S(2)}) copy-start(f32[256]{0:T(256)} %param.19) | copy-start | bytes 3076
  33.3 33.4 %copy-start.36 = (s32[1,4]{1,0:T(1,128)S(1)}, s32[1,4]{1,0:T(1,128)}, u32[]{:S(2)}) copy-start(s32[1,4]{1,0:T(1,128)} %param.17) | copy-start | bytes 52
  33.3 33.5 %copy-start.28 = (f32[256,128]{1,0:T(8,128)S(1)}, f32[256,128]{1,0:T(8,128)}, u32[]{:S(2)}) copy-start(f32[256,128]{1,0:T(8,128)} %param.21) | copy-start | bytes 393220
  33.3 21.8 %all-to-all-start = ((bf16[8,128,256]{2,1,0:T(8,128)(2,1)}), bf16[8,128,256]{2,1,0:T(8,128)(2,1)S(1)}, u32[]{:S(2)}, u32[]{:S(2)}) async-start(bf16[8,128,256]{2,1,0:T(8,128)(2,1)} %bitcast.5), calls=%async_computation | async-start | bytes 1048576 | tf_op jit(solution)/shard_map/all_to_all | solution.py:277
  39.8 43.5 %all-gather.19.cloned.1.call-start = ((), (), s32[]{:S(2)}) async-start(), calls=%async_computation.30 | async-start | bytes 1310720 | tf_op jit(solution)/shard_map/all_gather | solution.py:289
  57.7 52.9 %all-gather.11.cloned.1.call-start = ((), (), s32[]{:S(2)}) async-start(), calls=%async_computation.13 | async-start | bytes 1769472 | tf_op jit(solution)/shard_map/all_gather | solution.py:295
  58.5 142.6 %all-reduce.8.cloned.1.call-start = ((), (), s32[]{:S(2)}) async-start(), calls=%async_computation.14 | async-start | bytes 4194304 | tf_op jit(solution)/shard_map/psum | solution.py:328
  81.0 36.4 %copy-start.12 = (bf16[256,1024]{1,0:T(8,128)(2,1)}, bf16[256,1024]{1,0:T(8,128)(2,1)S(1)}, u32[]{:S(2)}) copy-start(bf16[256,1024]{1,0:T(8,128)(2,1)S(1)} %all_gather.42) | copy-start | bytes 1572868
  113.7 1.5 copy-start.16
  114.6 1.9 copy-start
  117.4 1.8 copy-start.24
  117.4 1.9 copy-start.25
  119.2 100.6 %all-gather.15.cloned.1.call-start = ((), (), s32[]{:S(2)}) async-start(), calls=%async_computation.16 | async-start | bytes 2359296 | tf_op jit(solution)/shard_map/all_gather | solution.py:296
  120.0 24.6 %copy-start.20 = (s32[512,4,32]{0,2,1:T(8,128)S(1)}, s32[512,4,32]{0,2,1:T(8,128)}, u32[]{:S(2)}) copy-start(s32[512,4,32]{0,2,1:T(8,128)} %param.18) | copy-start | bytes 786436
  120.1 135.8 %all-gather.21.cloned.1.call-start = ((), (), s32[]{:S(2)}) async-start(), calls=%async_computation.31 | async-start | bytes 1310720 | tf_op jit(solution)/shard_map/all_gather | solution.py:290
  123.5 22.2 %copy-start.35 = (f32[256]{0:T(256)S(1)}, f32[256]{0:T(256)}, u32[]{:S(2)}) copy-start(f32[256]{0:T(256)} %param.22) | copy-start | bytes 3076
  123.5 30.2 %copy-start.29 = (f32[128,256]{1,0:T(8,128)S(1)}, f32[128,256]{1,0:T(8,128)}, u32[]{:S(2)}) copy-start(f32[128,256]{1,0:T(8,128)} %param.26) | copy-start | bytes 393220
  142.0 27.6 %copy-start.30 = (f32[256,128]{1,0:T(8,128)S(1)}, f32[256,128]{1,0:T(8,128)}, u32[]{:S(2)}) copy-start(f32[256,128]{1,0:T(8,128)} %param.27) | copy-start | bytes 393220
  142.0 42.3 %copy-start.31 = (f32[2,32,512]{2,1,0:T(8,128)S(1)}, f32[2,32,512]{2,1,0:T(8,128)}, u32[]{:S(2)}) copy-start(f32[2,32,512]{2,1,0:T(8,128)} %param.24) | copy-start | bytes 393220
  144.6 138.2 %all-gather.13.cloned.1.call-start = ((), (), s32[]{:S(2)}) async-start(), calls=%async_computation.15 | async-start | bytes 2359296 | tf_op jit(solution)/shard_map/all_gather | solution.py:303
  145.5 177.4 %all-gather.17.cloned.1.call-start = ((), (), s32[]{:S(2)}) async-start(), calls=%async_computation.17 | async-start | bytes 3538944 | tf_op jit(solution)/shard_map/all_gather | solution.py:359
  153.7 47.5 %copy-start.4 = (bf16[512,1024]{1,0:T(8,128)(2,1)S(1)}, bf16[512,1024]{1,0:T(8,128)(2,1)}, u32[]{:S(2)}) copy-start(bf16[512,1024]{1,0:T(8,128)(2,1)} %all-gather.19.cloned.1.call-done) | copy-start | bytes 3145732
  203.1 1.4 copy-start.2
  204.7 48.9 %copy-start.6 = (bf16[512,1024]{1,0:T(8,128)(2,1)}, bf16[512,1024]{1,0:T(8,128)(2,1)S(1)}, u32[]{:S(2)}) copy-start(bf16[512,1024]{1,0:T(8,128)(2,1)S(1)} %multiply_convert_fusion.1) | copy-start | bytes 3145732
  219.8 3.9 copy-start.9
  222.7 1.0 copy-start.15
  259.5 254.8 %reduce-scatter.14.cloned.1.call-start = ((), (), s32[]{:S(2)}) async-start(), calls=%async_computation.20 | async-start | bytes 2359296 | tf_op jit(solution)/shard_map/reduce_scatter | solution.py:371
  322.9 2.9 copy-start.19
  479.5 80.0 %all-reduce.10.cloned.1.call-start = ((), (), s32[]{:S(2)}) async-start(), calls=%async_computation.21 | async-start | bytes 524288 | tf_op jit(solution)/shard_map/psum | solution.py:370
  516.1 95.6 %reduce-scatter.10.cloned.1.call-start = ((), (), s32[]{:S(2)}) async-start(), calls=%async_computation.18 | async-start | bytes 4718592 | tf_op jit(solution)/shard_map/reduce_scatter | solution.py:369
  516.7 167.8 %all-reduce.12.cloned.1.call-start = ((), (), s32[]{:S(2)}) async-start(), calls=%async_computation.22 | async-start | bytes 4194304 | tf_op jit(solution)/shard_map/psum | solution.py:410
  560.6 16.5 %copy-start.10 = (bf16[2,256,512]{2,1,0:T(8,128)(2,1)S(1)}, bf16[2,256,512]{2,1,0:T(8,128)(2,1)}, u32[]{:S(2)}) copy-start(bf16[2,256,512]{2,1,0:T(8,128)(2,1)} %all_gather.46) | copy-start | bytes 1572868
  577.1 4.9 copy-start.11
  577.1 2.2 copy-start.32
  577.6 1.0 copy-start.23
  579.3 32.4 %copy-start.22 = (f32[512,256]{1,0:T(8,128)S(1)}, f32[512,256]{1,0:T(8,128)}, u32[]{:S(2)}) copy-start(f32[512,256]{1,0:T(8,128)} %fusion.97) | copy-start | bytes 1572868
  579.3 32.4 %copy-start.26 = (f32[512,256]{1,0:T(8,128)S(1)}, f32[512,256]{1,0:T(8,128)}, u32[]{:S(2)}) copy-start(f32[512,256]{1,0:T(8,128)} %get-tuple-element.118) | copy-start | bytes 1572868
  582.0 31.0 %copy-start.8 = (bf16[1024,256]{1,0:T(8,128)(2,1)S(1)}, bf16[1024,256]{1,0:T(8,128)(2,1)}, u32[]{:S(2)}) copy-start(bf16[1024,256]{1,0:T(8,128)(2,1)} %all_gather.50) | copy-start | bytes 1572868
  613.0 3.6 copy-start.21
  616.5 68.0 %copy-start.3 = (f32[512,1024]{1,0:T(8,128)S(1)}, f32[512,1024]{1,0:T(8,128)}, u32[]{:S(2)}) copy-start(f32[512,1024]{1,0:T(8,128)} %copy-done.2) | copy-start | bytes 6291460
  616.6 103.1 %reduce-scatter.12.cloned.1.call-start = ((), (), s32[]{:S(2)}) async-start(), calls=%async_computation.19 | async-start | bytes 1310720 | tf_op jit(solution)/shard_map/reduce_scatter | solution.py:375
  619.5 168.6 %all-reduce.14.cloned.1.call-start = ((), (), s32[]{:S(2)}) async-start(), calls=%async_computation.23 | async-start | bytes 4194304 | tf_op jit(solution)/shard_map/psum | solution.py:432
  684.5 2.3 copy-start.7
  684.5 2.5 copy-start.14
  687.0 1.0 copy-start.13
  687.0 3.1 copy-start.1
  688.0 3.2 copy-start.5
  688.1 2.3 copy-start.17
  694.5 1.7 copy-start.33
  694.6 0.9 copy-start.18
  698.7 142.5 %reduce-scatter.22.cloned.1.call-start = ((), (), s32[]{:S(2)}) async-start(), calls=%async_computation.27 | async-start | bytes 1179648 | tf_op jit(solution)/shard_map/reduce_scatter | solution.py:444
  701.6 164.9 %reduce-scatter.24.cloned.1.call-start = ((), (), s32[]{:S(2)}) async-start(), calls=%async_computation.28 | async-start | bytes 1179648 | tf_op jit(solution)/shard_map/reduce_scatter | solution.py:441
  704.5 195.7 %reduce-scatter.26.cloned.1.call-start = ((), (), s32[]{:S(2)}) async-start(), calls=%async_computation.29 | async-start | bytes 1179648 | tf_op jit(solution)/shard_map/reduce_scatter | solution.py:443
  707.2 226.4 %reduce-scatter.18.cloned.1.call-start = ((), (), s32[]{:S(2)}) async-start(), calls=%async_computation.25 | async-start | bytes 1179648 | tf_op jit(solution)/shard_map/reduce_scatter | solution.py:442
  710.4 274.2 %reduce-scatter.20.cloned.1.call-start = ((), (), s32[]{:S(2)}) async-start(), calls=%async_computation.26 | async-start | bytes 4718592 | tf_op jit(solution)/shard_map/reduce_scatter | solution.py:440
  715.3 310.9 %reduce-scatter.16.cloned.1.call-start = ((), (), s32[]{:S(2)}) async-start(), calls=%async_computation.24 | async-start | bytes 3538944 | tf_op jit(solution)/shard_map/reduce_scatter | solution.py:439
  723.4 72.7 %all-to-all-start.2 = ((f32[8,128,256]{2,1,0:T(8,128)}), f32[8,128,256]{2,1,0:T(8,128)S(1)}, u32[]{:S(2)}, u32[]{:S(2)}) async-start(f32[8,128,256]{2,1,0:T(8,128)} %bitcast.148), calls=%async_computation.4 | async-start | bytes 2097152 | tf_op jit(solution)/shard_map/all_to_all | solution.py:449
  791.8 8.9 copy-start.37
  796.1 42.9 %all-to-all-start.3 = ((f32[8,128,256]{2,1,0:T(8,128)}), f32[8,128,256]{2,1,0:T(8,128)S(1)}, u32[]{:S(2)}, u32[]{:S(2)}) async-start(f32[8,128,256]{2,1,0:T(8,128)} %bitcast.40), calls=%async_computation.6 | async-start | bytes 2097152 | tf_op jit(solution)/shard_map/all_to_all | solution.py:456
Sparse Core Ops, SparseCore 0:
  57.9 25.3 all-gather.18
  85.5 25.0 all-gather.10
  119.3 69.1 all-reduce.7
  190.7 29.0 all-gather.14
  222.2 28.9 all-gather.20
  253.3 29.4 all-gather.12
  285.1 37.7 all-gather.16
  479.6 34.6 reduce-scatter.13
  518.0 41.4 all-reduce.9
  561.6 49.9 reduce-scatter.9
  616.7 67.7 all-reduce.11
  687.5 27.7 reduce-scatter.11
  718.4 69.6 all-reduce.13
  790.9 36.5 reduce-scatter.21
  830.3 36.2 reduce-scatter.23
  869.4 30.7 reduce-scatter.25
  903.0 30.6 reduce-scatter.17
  936.5 48.1 reduce-scatter.19
  987.6 38.4 reduce-scatter.15

commit v2 on v1

v2 whole, which is shorter than its diff:
```python
import functools

import jax
import jax.numpy as jnp
from jax import lax
from jax.experimental import pallas as pl
from jax.experimental.pallas import tpu as pltpu
from jax.sharding import PartitionSpec as P

D = 1024
HD = 64
MH = 4
QD = 512
NK = 256
PICKS = 32
LANES = 128
EPS = 1e-05
MASKED = -1e30
F32 = jnp.float32
LOW = jnp.bfloat16
MESH = pl.DeviceIdType.MESH
NT_DIMS = (((1,), (1,)), ((), ()))
VMEM_SPEC = pl.BlockSpec(memory_space=pltpu.VMEM)
VMEM_BYTES = 60 * 2**20


def flip(index, mask):
    bit = 1
    while bit <= mask:
        if mask & bit:
            index = index + bit - 2 * bit * (index // bit % 2)
        bit *= 2
    return index


class Net:
    def __init__(self, rows, cols, sends, recvs):
        self.rows, self.cols = rows, cols
        self.row, self.col = lax.axis_index("row"), lax.axis_index("col")
        self.sends, self.recvs, self.used = sends, recvs, 0
        self.pending = []

    def place(self, row_k, col_k):
        return (flip(self.row, row_k), flip(self.col, col_k))

    def meet(self, row_ks, col_ks):
        barrier = pltpu.get_barrier_semaphore()
        places = [self.place(k, 0) for k in row_ks] + [self.place(0, k) for k in col_ks]
        for place in places:
            pl.semaphore_signal(barrier, inc=1, device_id=place, device_id_type=MESH)
        pl.semaphore_wait(barrier, len(places))

    def send(self, src, dst, row_k=0, col_k=0):
        assert self.used < self.sends.shape[0]
        copy = pltpu.make_async_remote_copy(
            src_ref=src,
            dst_ref=dst,
            send_sem=self.sends.at[self.used],
            recv_sem=self.recvs.at[self.used],
            device_id=self.place(row_k, col_k),
            device_id_type=MESH,
        )
        copy.start()
        self.used += 1
        self.pending.append(copy)
        return copy

    def drain(self):
        for copy in self.pending:
            copy.wait_send()

    def gather_start(self, src, view, first=True):
        copies = [self.send(src, view(self.row), row_k=2 * j) for j in range(1, self.rows // 2)]
        return copies, self.send(src, view(self.row), row_k=1)

    def gather_pass(self, view, started):
        copies, sibling = started
        passed = []
        for j, copy in enumerate(copies):
            copy.wait_recv()
            there = flip(self.row, 2 * (j + 1))
            passed.append(self.send(view(there), view(there), row_k=1))
        return [sibling] + passed

    def scatter_start(self, view, across):
        twin = flip(self.row, 1)
        return [
            self.send(view(flip(twin, 2 * j)), across.at[j], row_k=1)
            for j in range(self.rows // 2)
        ]

    def scatter_pass(self, view, across, started, outgoing, incoming):
        moved = []
        for j in range(1, self.rows // 2):
            started[j].wait_recv()
            block = view(flip(self.row, 2 * j))[...] + across[j]
            outgoing[j - 1] = block.astype(outgoing.dtype)
            moved.append(self.send(outgoing.at[j - 1], incoming.at[j - 1], row_k=2 * j))
        return moved

    def scatter_end(self, view, across, started, incoming, moved):
        started[0].wait_recv()
        total = view(self.row)[...] + across[0]
        for j, copy in enumerate(moved):
            copy.wait_recv()
            total = total + incoming[j].astype(F32)
        return total

    def columns_start(self, view):
        return [self.send(view(self.col), view(self.col), col_k=k) for k in range(1, self.cols)]


def wait_all(copies):
    for copy in copies:
        copy.wait_recv()


def rows_of(ref, count):
    return lambda index: ref.at[pl.ds(pl.multiple_of(index * count, count), count), :]


def columns_of(ref, count):
    return lambda index: ref.at[:, pl.ds(pl.multiple_of(index * count, count), count)]


def one_hot_rows(positions, slots):
    places = lax.broadcasted_iota(jnp.int32, (positions.shape[0], slots), 1)
    return jnp.where(positions == places, 1.0, 0.0).astype(LOW)


def one_hot_columns(positions, slots):
    places = lax.broadcasted_iota(jnp.int32, (slots, positions.shape[1]), 0)
    return jnp.where(positions == places, 1.0, 0.0).astype(LOW)


def pack_for_rows(net, packed, values, positions):
    slots = packed.shape[0]
    packed[...] = jnp.dot(
        one_hot_columns(positions, slots), values, preferred_element_type=F32
    ).astype(LOW)


def exchange_start(net, packed, got, capacity):
    mine = rows_of(got, capacity)
    theirs = rows_of(packed, capacity)
    copies = [
        net.send(theirs(flip(net.row, k)), mine(net.row), row_k=k) for k in range(1, net.rows)
    ]
    mine(net.row)[...] = theirs(net.row)[...]
    return copies


def unpack(got, positions):
    return jnp.dot(
        one_hot_rows(positions, got.shape[0]), got[...], preferred_element_type=F32
    )


def share_sums(net, sums, mine, theirs):
    tokens = sums.shape[0]
    mine[...] = jnp.broadcast_to(sums, (tokens, LANES)).T[:8]
    copies = [net.send(mine, theirs.at[k], col_k=k) for k in range(1, net.cols)]
    wait_all(copies)
    total = mine[...]
    for k in range(1, net.cols):
        total = total + theirs[k]
    return jnp.broadcast_to(total[:1], (LANES, tokens)).T


def widen(lanes, width):
    return jnp.concatenate([lanes] * (width // LANES), axis=1)


def reduce_start(net, part, outgoing, incoming):
    width = part.shape[1] // net.cols
    view = columns_of(part, width)
    copies = []
    for k in range(1, net.cols):
        outgoing[k - 1] = view(flip(net.col, k))[...].astype(LOW)
        copies.append(net.send(outgoing.at[k - 1], incoming.at[k - 1], col_k=k))
    return copies


def reduce_end(net, part, incoming, copies):
    total = columns_of(part, part.shape[1] // net.cols)(net.col)[...].astype(F32)
    for k, copy in enumerate(copies):
        copy.wait_recv()
        total = total + incoming[k].astype(F32)
    return total


def deal_kernel(
    rows, cols, tokens_ref, send_row, recv_col, shard, full, weights, packed, got, sends, recvs
):
    net = Net(rows, cols, sends, recvs)
    capacity = packed.shape[0] // rows
    pack_for_rows(net, packed, tokens_ref[...], send_row[...])
    net.meet(range(1, rows), range(1, cols))
    copies = exchange_start(net, packed, got, capacity)
    count = shard.shape[0]
    place = rows_of(weights, count)
    gather = net.gather_start(shard, place)
    place(net.row)[...] = shard[...]
    wait_all(copies)
    mine = columns_of(full, tokens_ref.shape[1])
    mine(net.col)[...] = unpack(got, recv_col[...]).astype(LOW)
    spread = net.columns_start(mine)
    wait_all(net.gather_pass(place, gather))
    wait_all(spread)
    net.drain()


def norm_kernel(
    rows,
    cols,
    part,
    dealt,
    gain,
    cot,
    send_row,
    recv_col,
    shard,
    keys,
    picks,
    hidden,
    resid,
    factor,
    full,
    weights,
    key_table,
    all_picks,
    packed,
    got,
    outgoing,
    incoming,
    mine,
    theirs,
    sends,
    recvs,
):
    net = Net(rows, cols, sends, recvs)
    capacity = packed.shape[0] // rows
    width = dealt.shape[1]
    net.meet(range(1, rows), range(1, cols))
    reduce = reduce_start(net, part, outgoing, incoming)
    pack_for_rows(net, packed, cot[...], send_row[...])
    copies = exchange_start(net, packed, got, capacity)
    place = rows_of(weights, shard.shape[0])
    gather = net.gather_start(shard, place)
    span = keys.shape[1]
    key_place = lambda index: key_table.at[:, pl.ds(pl.multiple_of(index * span, span), span), :]
    key_gather = net.gather_start(keys, key_place)
    pick_place = rows_of(all_picks, picks.shape[0])
    pick_gather = net.gather_start(picks, pick_place)
    place(net.row)[...] = shard[...]
    key_place(net.row)[...] = keys[...]
    pick_place(net.row)[...] = picks[...]
    values = dealt[...] + reduce_end(net, part, incoming, reduce)
    resid[...] = values
    square = share_sums(net, jnp.sum(values * values, axis=1, keepdims=True), mine, theirs)
    scale = lax.rsqrt(square / D + EPS)
    factor[...] = scale
    own = columns_of(hidden, width)
    own(net.col)[...] = (resid[...] * widen(scale, width) * gain[...]).astype(LOW)
    spread = net.columns_start(own)
    wait_all(copies)
    own_cot = columns_of(full, width)
    own_cot(net.col)[...] = unpack(got, recv_col[...]).astype(LOW)
    cot_spread = net.columns_start(own_cot)
    left = net.gather_pass(place, gather)
    left += net.gather_pass(key_place, key_gather)
    left += net.gather_pass(pick_place, pick_gather)
    wait_all(spread)
    wait_all(cot_spread)
    wait_all(left)
    net.drain()


def score_kernel(
    rows, cols, part, grads, weights, all_low, all_grads, scores, sends, recvs
):
    net = Net(rows, cols, sends, recvs)
    net.meet([1] + [2 * j for j in range(1, rows // 2)], range(1, cols))
    place = rows_of(scores, part.shape[0])
    copies = [net.send(part, place(net.col), col_k=k) for k in range(1, cols)]
    grad_place = rows_of(all_grads, grads.shape[0])
    grad_gather = net.gather_start(grads, grad_place)
    place(net.col)[...] = part[...]
    grad_place(net.row)[...] = grads[...]
    wait_all(copies)
    low_place = lambda index: all_low.at[index]
    for m in range(MH):
        score = (
            scores[2 * m * PICKS : (2 * m + 1) * PICKS]
            + scores[(2 * m + 1) * PICKS : (2 * m + 2) * PICKS]
        )
        shifted = jnp.exp(score - jnp.max(score, axis=0, keepdims=True))
        share = shifted / jnp.sum(shifted, axis=0, keepdims=True)
        weights[m * PICKS : (m + 1) * PICKS] = share
    low_place(net.row)[...] = weights[...].astype(LOW)
    low_gather = net.gather_start(low_place(net.row), low_place)
    left = net.gather_pass(grad_place, grad_gather)
    left += net.gather_pass(low_place, low_gather)
    wait_all(left)
    net.drain()


def memory_sum_kernel(
    rows,
    cols,
    mem_part,
    dw_part,
    memory,
    dw,
    mem_across,
    mem_out,
    mem_in,
    dw_across,
    dw_sum,
    dw_cols,
    dw_out,
    dw_in,
    sends,
    recvs,
):
    net = Net(rows, cols, sends, recvs)
    tokens = memory.shape[0]
    half = rows // 2
    net.meet([1] + [2 * j for j in range(1, half)], range(1, cols))
    dw_view = lambda index: dw_part.at[index]
    dw_started = net.scatter_start(dw_view, dw_across)
    mem_view = rows_of(mem_part, tokens)
    mem_started = net.scatter_start(mem_view, mem_across)
    for j in range(half):
        dw_started[j].wait_recv()
        dw_sum[j] = dw_view(flip(net.row, 2 * j))[...] + dw_across[j]
    head = lambda col: pl.ds(pl.multiple_of(col * MH // cols * PICKS, PICKS), PICKS)
    moved = [
        net.send(dw_sum.at[:, head(flip(net.col, k)), :], dw_cols.at[k - 1], col_k=k)
        for k in range(1, cols)
    ]
    mem_moved = net.scatter_pass(mem_view, mem_across, mem_started, mem_out, mem_in)
    wait_all(moved)
    for j in range(half):
        total = dw_sum[j, head(net.col), :]
        for k in range(1, cols):
            total = total + dw_cols[k - 1, j]
        dw_out[j] = total
    last = [
        net.send(dw_out.at[j], dw_in.at[j - 1], row_k=2 * j) for j in range(1, half)
    ]
    memory[...] = net.scatter_end(mem_view, mem_across, mem_started, mem_in, mem_moved)
    total = dw_out[0]
    for j, copy in enumerate(last):
        copy.wait_recv()
        total = total + dw_in[j]
    dw[...] = total
    net.drain()


def norm_grad(net, grad_hidden, values, scale, gain, extra, mine, theirs):
    width = values.shape[1]
    scaled = grad_hidden * gain
    inner = share_sums(net, jnp.sum(scaled * values, axis=1, keepdims=True), mine, theirs)
    wide = widen(scale, width)
    grads = wide * scaled - values * (wide * wide * wide) * widen(inner, width) / D
    grad_gain = jnp.sum(grad_hidden * values * wide, axis=0, keepdims=True)
    return grads + extra, grad_gain


def back_two_kernel(
    rows,
    cols,
    part,
    result_part,
    resid,
    factor,
    gain,
    cot,
    recv_row,
    send_col,
    weight_grad,
    key_grad,
    grad_low,
    grad_resid,
    result,
    own_weight,
    own_keys,
    gain_grad,
    outgoing,
    incoming,
    res_outgoing,
    res_incoming,
    mine,
    theirs,
    packed,
    got,
    across,
    w_out,
    w_in,
    k_across,
    k_out,
    k_in,
    sends,
    recvs,
):
    net = Net(rows, cols, sends, recvs)
    capacity = packed.shape[0] // rows
    width = resid.shape[1]
    net.meet(range(1, rows), range(1, cols))
    reduce = reduce_start(net, part, outgoing, incoming)
    res_reduce = reduce_start(net, result_part, res_outgoing, res_incoming)
    view = rows_of(weight_grad, own_weight.shape[0])
    span = own_keys.shape[1]
    key_view = lambda index: key_grad.at[:, pl.ds(pl.multiple_of(index * span, span), span), :]
    started = net.scatter_start(view, across)
    key_started = net.scatter_start(key_view, k_across)
    grad_hidden = reduce_end(net, part, incoming, reduce)
    grads, gain_sum = norm_grad(
        net, grad_hidden, resid[...], factor[...], gain[...], cot[...].astype(F32), mine, theirs
    )
    grad_resid[...] = grads
    gain_grad[...] = jnp.broadcast_to(gain_sum, gain_grad.shape)
    own = columns_of(grad_low, width)
    own(net.col)[...] = grads.astype(LOW)
    spread = net.columns_start(own)
    block = resid[...] + reduce_end(net, result_part, res_incoming, res_reduce)
    pack_for_rows(net, packed, block.astype(LOW), recv_row[...])
    copies = exchange_start(net, packed, got, capacity)
    moved = net.scatter_pass(view, across, started, w_out, w_in)
    key_moved = net.scatter_pass(key_view, k_across, key_started, k_out, k_in)
    wait_all(copies)
    result[...] = unpack(got, send_col[...])
    own_weight[...] = net.scatter_end(view, across, started, w_in, moved)
    own_keys[...] = net.scatter_end(key_view, k_across, key_started, k_in, key_moved)
    wait_all(spread)
    net.drain()


def back_one_kernel(
    rows,
    cols,
    part,
    dealt,
    factor,
    gain,
    extra,
    recv_row,
    send_col,
    weight_grad,
    gain_two,
    result,
    own_weight,
    gains,
    outgoing,
    incoming,
    mine,
    theirs,
    packed,
    got,
    across,
    w_out,
    w_in,
    my_gains,
    their_gains,
    sends,
    recvs,
):
    net = Net(rows, cols, sends, recvs)
    capacity = packed.shape[0] // rows
    net.meet(range(1, rows), range(1, cols))
    reduce = reduce_start(net, part, outgoing, incoming)
    view = rows_of(weight_grad, own_weight.shape[0])
    started = net.scatter_start(view, across)
    grad_hidden = reduce_end(net, part, incoming, reduce)
    grads, gain_sum = norm_grad(
        net, grad_hidden, dealt[...], factor[...], gain[...], extra[...], mine, theirs
    )
    pack_for_rows(net, packed, grads.astype(LOW), recv_row[...])
    copies = exchange_start(net, packed, got, capacity)
    places = lax.broadcasted_iota(jnp.int32, my_gains.shape, 0)
    my_gains[...] = jnp.where(places == 0, gain_sum, gain_two[...])
    gain_copies = [
        net.send(my_gains, their_gains.at[k], row_k=k) for k in range(1, rows)
    ]
    moved = net.scatter_pass(view, across, started, w_out, w_in)
    wait_all(copies)
    result[...] = unpack(got, send_col[...])
    total = my_gains[...]
    for k, copy in enumerate(gain_copies):
        copy.wait_recv()
        total = total + their_gains[k + 1]
    gains[...] = total
    own_weight[...] = net.scatter_end(view, across, started, w_in, moved)
    net.drain()


def remote_call(kernel, rows, cols, number, copies, ins, outs, scratch):
    return pl.pallas_call(
        functools.partial(kernel, rows, cols),
        out_shape=[jax.ShapeDtypeStruct(shape, dtype) for shape, dtype in outs],
        in_specs=[VMEM_SPEC] * len(ins),
        out_specs=[VMEM_SPEC] * len(outs),
        scratch_shapes=[pltpu.VMEM(shape, dtype) for shape, dtype in scratch]
        + [pltpu.SemaphoreType.DMA((copies,)), pltpu.SemaphoreType.DMA((copies,))],
        compiler_params=pltpu.CompilerParams(
            collective_id=number, has_side_effects=True, vmem_limit_bytes=VMEM_BYTES
        ),
    )(*ins)


def plain_call(kernel, ins, outs):
    return pl.pallas_call(
        kernel,
        out_shape=[jax.ShapeDtypeStruct(shape, dtype) for shape, dtype in outs],
        in_specs=[VMEM_SPEC] * len(ins),
        out_specs=[VMEM_SPEC] * len(outs),
        compiler_params=pltpu.CompilerParams(vmem_limit_bytes=VMEM_BYTES),
    )(*ins)


def middle_kernel(
    halves, hidden, weights, keys, cot, index, queries, gate, grad_mixed, grad_memory, part
):
    width = gate.shape[1]
    depth = halves * QD
    for h in range(halves):
        columns = slice(h * QD, (h + 1) * QD)
        queries[:, columns] = jnp.dot(
            hidden[...], weights[:, columns], preferred_element_type=F32
        ).astype(LOW)
    open_gate = jnp.dot(
        hidden[...], weights[:, depth : depth + width], preferred_element_type=F32
    )
    gate[...] = open_gate
    back = jnp.dot(cot[...], weights[:, depth + width :], preferred_element_type=F32)
    grad_mixed[...] = back
    grad_memory[...] = (back * (open_gate * jax.nn.sigmoid(open_gate))).astype(LOW)
    lanes = lax.broadcasted_iota(jnp.int32, index.shape, 1)
    low_index = index[...] % LANES
    upper = index[...] >= LANES
    found = jnp.zeros(index.shape, F32)
    for h in range(halves):
        scores = lax.dot_general(
            queries[:, h * QD : (h + 1) * QD], keys[h], NT_DIMS, preferred_element_type=F32
        )
        first = jnp.take_along_axis(scores[:, :LANES], low_index, axis=1)
        second = jnp.take_along_axis(scores[:, LANES:], low_index, axis=1)
        found = jnp.where(lanes // PICKS == h, jnp.where(upper, second, first), found)
    part[...] = found.T[: halves * PICKS]


def spread_kernel(halves, weights, dw, index, out):
    tokens = weights.shape[1]
    change = dw[...]
    share = weights[...]
    grad = share * (change - jnp.sum(share * change, axis=0, keepdims=True))
    block = 128
    places = lax.broadcasted_iota(jnp.int32, (NK, block), 0)
    for h in range(halves):
        for b in range(tokens // block):
            columns = slice(b * block, (b + 1) * block)
            total = jnp.zeros((NK, block), F32)
            for k in range(PICKS):
                row = index[h * PICKS + k : h * PICKS + k + 1, columns]
                total = total + jnp.where(places == row, grad[k : k + 1, columns], 0.0)
            out[columns, h * NK : (h + 1) * NK] = total.T.astype(LOW)


def memory_kernel(
    groups, tok_block, iters, picks_ref, w_ref, dm_ref, table_ref, mem_ref, dw_ref, gt_ref, dense, gacc, hi_ref, lo_ref, wide_ref, found_ref
):
    spans = groups * NK // LANES
    pitch = spans + 8
    per_tok = tok_block // iters
    per_span = spans // iters
    step = pl.program_id(0)

    @pl.when(step == 0)
    def _():
        gacc[...] = jnp.zeros_like(gacc)

    picks = picks_ref[...].astype(jnp.int32) + 32768
    hi_ref[...] = (picks // LANES - lax.axis_index("row") * spans).astype(F32)
    lo_ref[...] = (picks % LANES).astype(F32)
    wide_ref[...] = w_ref[0].astype(F32).T
    places_lo = lax.broadcasted_iota(jnp.int32, (LANES, LANES), 0).astype(F32).astype(LOW)
    places_hi = lax.broadcasted_iota(jnp.int32, (spans, LANES), 0).astype(F32).astype(LOW)
    ones = jnp.ones((LANES, LANES), LOW)
    zeros = jnp.zeros((LANES, LANES), LOW)
    blank = jnp.zeros((spans, LANES), LOW)
    grads = dm_ref[...]
    grads_t = grads.T
    mem_ref[...] = jnp.zeros_like(mem_ref)
    found_ref[...] = jnp.zeros_like(found_ref)
    lo_int = picks % LANES
    hi_all = hi_ref[...]

    def token_pair(first):
        rights, lefts = [], []
        for token in (first, first + 1):
            lo_row = jnp.broadcast_to(lo_ref[pl.ds(token, 1), :], (LANES, LANES)).astype(LOW)
            hi_row = jnp.broadcast_to(hi_ref[pl.ds(token, 1), :], (spans, LANES)).astype(LOW)
            w_row = jnp.broadcast_to(wide_ref[pl.ds(token, 1), :], (spans, LANES)).astype(LOW)
            rights.append(jnp.where(lo_row == places_lo, ones, zeros))
            lefts.append(jnp.where(hi_row == places_hi, w_row, blank))
        right = jnp.concatenate(rights, axis=1)
        left = jnp.concatenate(
            [
                jnp.concatenate([lefts[0], blank], axis=1),
                jnp.concatenate([blank, lefts[1]], axis=1),
            ],
            axis=0,
        )
        both = lax.dot_general(left, right, NT_DIMS, preferred_element_type=F32)
        for j in range(2):
            dense[pl.ds(pl.multiple_of((first + j) * pitch, 8), spans), :] = both[
                j * spans : (j + 1) * spans
            ]

    def build(it, _):
        rows = pl.ds(pl.multiple_of(it * per_span * LANES, LANES), per_span * LANES)
        products = lax.dot_general(grads, table_ref[rows, :], NT_DIMS, preferred_element_type=F32)
        found = found_ref[...]
        pairs = per_tok // 2 // per_span
        for j in range(per_span):
            picked = jnp.take_along_axis(products[:, LANES * j : LANES * (j + 1)], lo_int, axis=1)
            found = jnp.where(hi_all == (it * per_span + j).astype(F32), picked, found)
            for u in range(pairs):
                token_pair(it * per_tok + (j * pairs + u) * 2)
        found_ref[...] = found
        return 0

    lax.fori_loop(0, iters, build, 0)
    dw_ref[0] = found_ref[...].T

    def multiply(it, _):
        rows = pl.ds(pl.multiple_of(it * per_span * LANES, LANES), per_span * LANES)
        weights = jnp.concatenate(
            [
                dense[pl.ds(it * per_span + j, tok_block, stride=pitch), :].astype(LOW)
                for j in range(per_span)
            ],
            axis=1,
        )
        mem_ref[...] += jnp.dot(weights, table_ref[rows, :], preferred_element_type=F32)
        gacc[:, rows] += jnp.dot(grads_t, weights, preferred_element_type=F32)
        return 0

    lax.fori_loop(0, iters, multiply, 0)

    @pl.when(step == pl.num_programs(0) - 1)
    def _():
        def turn(i, _):
            rows = pl.ds(pl.multiple_of(i * NK, NK), NK)
            gt_ref[rows, :] = gacc[:, rows].T
            return 0

        lax.fori_loop(0, groups, turn, 0)


def memory_call(picks, weights, grads, table):
    tokens, count = picks.shape
    rows, width = table.shape
    groups = rows // NK
    block = weights.shape[2]
    spec = lambda n: pl.BlockSpec((block, n), lambda i: (i, 0))
    turned = pl.BlockSpec((1, count, block), lambda i: (i, 0, 0))
    return pl.pallas_call(
        functools.partial(memory_kernel, groups, block, 4),
        grid=(tokens // block,),
        in_specs=[spec(count), turned, spec(width), pl.BlockSpec((rows, width), lambda i: (0, 0))],
        out_specs=[
            spec(width),
            turned,
            pl.BlockSpec((rows, width), lambda i: (0, 0), pipeline_mode=pl.Buffered(1)),
        ],
        out_shape=[
            jax.ShapeDtypeStruct((tokens, width), F32),
            jax.ShapeDtypeStruct((tokens // block, count, block), F32),
            jax.ShapeDtypeStruct((rows, width), F32),
        ],
        scratch_shapes=[
            pltpu.VMEM((block * (rows // LANES + 8), LANES), F32),
            pltpu.VMEM((width, rows), F32),
        ]
        + [pltpu.VMEM((block, count), F32)] * 4,
        compiler_params=pltpu.CompilerParams(vmem_limit_bytes=62 * 2**20),
    )(picks, weights, grads, table)


def attention_forward(queries, key_rows, value_rows, allowed, score_scale):
    scores = (
        jnp.einsum("qhd,khd->hqk", queries, key_rows, preferred_element_type=F32) * score_scale
    )
    scores = jnp.where(allowed[None], scores, MASKED)
    row_max = jnp.max(scores, axis=2, keepdims=True)
    shifted_exp = jnp.exp(scores - row_max)
    row_total = jnp.sum(shifted_exp, axis=2, keepdims=True)
    weights_low = (shifted_exp / row_total).astype(LOW)
    weighted = jnp.einsum("hqk,khd->qhd", weights_low, value_rows, preferred_element_type=F32)
    mixed = weighted.astype(LOW).reshape(queries.shape[0], -1)
    return mixed, row_max + jnp.log(row_total)


def attention_backward(queries, key_rows, value_rows, grad_out, log_total, allowed, score_scale):
    scores = (
        jnp.einsum("qhd,khd->hqk", queries, key_rows, preferred_element_type=F32) * score_scale
    )
    scores = jnp.where(allowed[None], scores, MASKED)
    probs = jnp.exp(scores - log_total)
    grad_prob = jnp.einsum("qhd,khd->hqk", grad_out, value_rows, preferred_element_type=F32)
    inner = jnp.sum(probs * grad_prob, axis=2, keepdims=True)
    grad_score = (probs * (grad_prob - inner)).astype(LOW)
    query_grad = (
        jnp.einsum("hqk,khd->qhd", grad_score, key_rows, preferred_element_type=F32) * score_scale
    )
    key_grad = (
        jnp.einsum("hqk,qhd->khd", grad_score, queries, preferred_element_type=F32) * score_scale
    )
    value_grad = jnp.einsum(
        "hqk,qhd->khd", probs.astype(LOW), grad_out, preferred_element_type=F32
    )
    return query_grad, key_grad, value_grad


def per_device(
    tokens,
    cotangent,
    deal_order,
    seq_lengths,
    value_picks,
    norm1_gain,
    w_qkv,
    w_attn_out,
    norm2_gain,
    w_query,
    sub_keys,
    value_table,
    w_gate,
    w_mem_out,
):
    rows, cols = lax.axis_size("row"), lax.axis_size("col")
    row_index, col_index = lax.axis_index("row"), lax.axis_index("col")
    count, width = tokens.shape
    capacity = 2 * count // rows
    slots = rows * capacity
    shard_rows = w_qkv.shape[0]
    heads_here = width // HD
    halves = sub_keys.shape[0]
    depth = halves * QD
    score_scale = HD ** (-0.5)

    my_slots = lax.dynamic_slice_in_dim(deal_order, row_index * count, count)
    source = my_slots // count
    from_source = (source[:, None] == jnp.arange(rows, dtype=jnp.int32)[None, :]).astype(jnp.int32)
    earlier = jnp.cumsum(from_source, axis=0) - from_source
    recv_pos = source * capacity + jnp.sum(earlier * from_source, axis=1)
    owned = (deal_order // count == row_index).astype(jnp.int32).reshape(rows, count)
    rank = jnp.cumsum(owned, axis=1) - owned
    slot_pos = (jnp.arange(rows, dtype=jnp.int32)[:, None] * capacity + rank).reshape(-1)
    mine = (deal_order - row_index * count)[None, :] == jnp.arange(count, dtype=jnp.int32)[:, None]
    send_pos = jnp.sum(jnp.where(mine, slot_pos[None, :], 0), axis=1)
    send_row, send_col = send_pos[None, :], send_pos[:, None]
    recv_row, recv_col = recv_pos[None, :], recv_pos[:, None]

    shard_one = jnp.concatenate([w_qkv.astype(LOW), w_attn_out.astype(LOW).T], axis=1)
    shard_two = jnp.concatenate(
        [w_query.astype(LOW), w_gate.astype(LOW), w_mem_out.astype(LOW).T], axis=1
    )
    gain_one = norm1_gain.astype(LOW).astype(F32)[None, :]
    gain_two = norm2_gain.astype(LOW).astype(F32)[None, :]
    gain_all = lax.all_gather(norm1_gain.astype(LOW), "col", axis=0, tiled=True).astype(F32)
    swap = [((slots, width), LOW), ((slots, width), LOW)]

    full_tokens, weights_one = remote_call(
        deal_kernel,
        rows,
        cols,
        0,
        rows - 1 + cols - 1 + rows,
        [tokens, send_row, recv_col, shard_one],
        [((count, D), LOW), ((D, shard_one.shape[1]), LOW)],
        swap,
    )
    qkv_weight, attn_weight = weights_one[:, : 3 * width], weights_one[:, 3 * width :]
    dealt = full_tokens.astype(F32)
    factor_one = lax.rsqrt(jnp.mean(dealt * dealt, axis=1, keepdims=True) + EPS)
    hidden_one = (dealt * factor_one * gain_all).astype(LOW)
    dealt_own = lax.dynamic_slice_in_dim(dealt, col_index * width, width, 1)

    places = jnp.arange(count, dtype=jnp.int32)
    seq_ids = jnp.sum(
        (places[:, None] >= jnp.cumsum(seq_lengths[0])[None, :]).astype(jnp.int32), axis=1
    )
    allowed = (seq_ids[:, None] == seq_ids[None, :]) & (places[:, None] >= places[None, :])
    qkv = (
        jnp.dot(hidden_one, qkv_weight, preferred_element_type=F32)
        .astype(LOW)
        .reshape(count, heads_here, 3, HD)
    )
    queries, key_rows, value_rows = qkv[:, :, 0, :], qkv[:, :, 1, :], qkv[:, :, 2, :]
    mixed, log_total = attention_forward(queries, key_rows, value_rows, allowed, score_scale)
    attn_part = lax.dot_general(mixed, attn_weight, NT_DIMS, preferred_element_type=F32)

    flat_picks = value_picks.reshape(count, MH * PICKS)
    sums = [
        ((cols - 1, count, width), LOW),
        ((cols - 1, count, width), LOW),
        ((8, count), F32),
        ((cols, 8, count), F32),
    ]
    hidden_two, resid, factor_two, full_cot, weights_two, key_table, all_picks = remote_call(
        norm_kernel,
        rows,
        cols,
        1,
        rows - 1 + 4 * (cols - 1) + 3 * rows,
        [
            attn_part,
            dealt_own,
            gain_two,
            cotangent,
            send_row,
            recv_col,
            shard_two,
            sub_keys.astype(LOW),
            (flat_picks - 32768).astype(jnp.int16),
        ],
        [
            ((count, D), LOW),
            ((count, width), F32),
            ((count, LANES), F32),
            ((count, D), LOW),
            ((D, shard_two.shape[1]), LOW),
            ((halves, NK, QD), LOW),
            ((rows * count, MH * PICKS), jnp.int16),
        ],
        swap + sums,
    )
    half_ids = col_index * halves + jnp.arange(halves, dtype=jnp.int32)
    head = half_ids[0] // 2
    head_picks = lax.dynamic_index_in_dim(value_picks, head, 1, keepdims=False)
    sub_index = jnp.concatenate(
        [
            jnp.where(half_ids[h] % 2 == 0, head_picks // NK, head_picks % NK)
            for h in range(halves)
        ],
        axis=1,
    )
    padded_index = jnp.pad(sub_index, ((0, 0), (0, LANES - halves * PICKS)))
    mem_queries, gate, grad_mixed, grad_memory, score_part = plain_call(
        functools.partial(middle_kernel, halves),
        [hidden_two, weights_two, key_table, full_cot, padded_index],
        [
            ((count, depth), LOW),
            ((count, width), F32),
            ((count, width), F32),
            ((count, width), LOW),
            ((halves * PICKS, count), F32),
        ],
    )
    pick_weights, all_low, all_grads = remote_call(
        score_kernel,
        rows,
        cols,
        2,
        cols - 1 + 2 * rows,
        [score_part, grad_memory],
        [
            ((MH * PICKS, count), F32),
            ((rows, MH * PICKS, count), LOW),
            ((rows * count, width), LOW),
        ],
        [((2 * MH * PICKS, count), F32)],
    )
    mem_part, dw_part, grad_table = memory_call(
        all_picks, all_low, all_grads, value_table.astype(LOW)
    )
    half = rows // 2
    memory, grad_pick = remote_call(
        memory_sum_kernel,
        rows,
        cols,
        3,
        2 * half + 2 * (half - 1) + cols - 1,
        [mem_part, dw_part],
        [((count, width), F32), ((PICKS, count), F32)],
        [
            ((half, count, width), F32),
            ((half - 1, count, width), LOW),
            ((half - 1, count, width), LOW),
            ((half, MH * PICKS, count), F32),
            ((half, MH * PICKS, count), F32),
            ((cols - 1, half, PICKS, count), F32),
            ((half, PICKS, count), F32),
            ((half - 1, PICKS, count), F32),
        ],
    )
    own_weights = lax.dynamic_slice_in_dim(pick_weights, head * PICKS, PICKS, 0)
    (grad_sub,) = plain_call(
        functools.partial(spread_kernel, halves),
        [own_weights, grad_pick, sub_index.T],
        [((count, halves * NK), LOW)],
    )
    sigmoid_gate = jax.nn.sigmoid(gate)
    mixed_two = (memory * gate * sigmoid_gate).astype(LOW)
    grad_gate = (
        grad_mixed * memory * sigmoid_gate * (1.0 + gate * (1.0 - sigmoid_gate))
    ).astype(LOW)
    memout_part = lax.dot_general(
        mixed_two, weights_two[:, depth + width :], NT_DIMS, preferred_element_type=F32
    )
    grad_sub = grad_sub.reshape(count, halves, NK)
    grad_queries = (
        jnp.einsum("tnj,njq->tnq", grad_sub, key_table, preferred_element_type=F32)
        .astype(LOW)
        .reshape(count, depth)
    )
    grad_keys = jnp.einsum(
        "tnj,tnq->njq",
        grad_sub,
        mem_queries.reshape(count, halves, QD),
        preferred_element_type=F32,
    )
    grad_both = jnp.concatenate([grad_queries, grad_gate], axis=1)
    hidden_two_part = lax.dot_general(
        grad_both, weights_two[:, : depth + width], NT_DIMS, preferred_element_type=F32
    )
    grad_two = jnp.concatenate(
        [
            jnp.einsum("tD,tm->Dm", hidden_two, grad_both, preferred_element_type=F32),
            jnp.einsum("tD,tc->Dc", full_cot, mixed_two, preferred_element_type=F32),
        ],
        axis=1,
    )
    own_cot = lax.dynamic_slice_in_dim(full_cot, col_index * width, width, 1)
    grad_low, grad_resid, output, own_two, own_keys, gain_two_part = remote_call(
        back_two_kernel,
        rows,
        cols,
        4,
        4 * (cols - 1) + rows - 1 + 2 * (half + half - 1),
        [
            hidden_two_part,
            memout_part,
            resid,
            factor_two,
            gain_two,
            own_cot,
            recv_row,
            send_col,
            grad_two,
            grad_keys,
        ],
        [
            ((count, D), LOW),
            ((count, width), F32),
            ((count, width), F32),
            (shard_two.shape, F32),
            (sub_keys.shape, F32),
            ((8, width), F32),
        ],
        [
            ((cols - 1, count, width), LOW),
            ((cols - 1, count, width), LOW),
            *sums,
            *swap,
            ((half,) + shard_two.shape, F32),
            ((half - 1,) + shard_two.shape, LOW),
            ((half - 1,) + shard_two.shape, LOW),
            ((half,) + sub_keys.shape, F32),
            ((half - 1,) + sub_keys.shape, LOW),
            ((half - 1,) + sub_keys.shape, LOW),
        ],
    )
    grad_heads = (
        jnp.dot(grad_low, attn_weight, preferred_element_type=F32)
        .astype(LOW)
        .reshape(count, heads_here, HD)
    )
    grad_qkv = (
        jnp.stack(
            attention_backward(
                queries, key_rows, value_rows, grad_heads, log_total, allowed, score_scale
            ),
            axis=2,
        )
        .astype(LOW)
        .reshape(count, heads_here * 3 * HD)
    )
    grad_one = jnp.concatenate(
        [
            jnp.einsum("tD,tm->Dm", hidden_one, grad_qkv, preferred_element_type=F32),
            jnp.einsum("tD,tc->Dc", grad_low, mixed, preferred_element_type=F32),
        ],
        axis=1,
    )
    hidden_one_part = lax.dot_general(grad_qkv, qkv_weight, NT_DIMS, preferred_element_type=F32)
    grad_tokens, own_one, gains = remote_call(
        back_one_kernel,
        rows,
        cols,
        5,
        2 * (cols - 1) + 2 * (rows - 1) + half + half - 1,
        [
            hidden_one_part,
            dealt_own,
            jnp.broadcast_to(factor_one, (count, LANES)),
            gain_one,
            grad_resid,
            recv_row,
            send_col,
            grad_one,
            gain_two_part,
        ],
        [((count, width), F32), (shard_one.shape, F32), ((8, width), F32)],
        [
            *sums,
            *swap,
            ((half,) + shard_one.shape, F32),
            ((half - 1,) + shard_one.shape, LOW),
            ((half - 1,) + shard_one.shape, LOW),
            ((8, width), F32),
            ((rows, 8, width), F32),
        ],
    )
    gain_span = width // rows
    gain_one_grad = lax.dynamic_slice_in_dim(gains[0], row_index * gain_span, gain_span)
    gain_two_grad = lax.dynamic_slice_in_dim(gains[1], row_index * gain_span, gain_span)
    return (
        output,
        grad_tokens,
        gain_one_grad,
        own_one[:, : 3 * width],
        own_one[:, 3 * width :].T,
        gain_two_grad,
        own_two[:, :depth],
        own_keys,
        grad_table,
        own_two[:, depth : depth + width],
        own_two[:, depth + width :].T,
    )


def solution(mesh):
    return jax.shard_map(
        per_device,
        mesh=mesh,
        in_specs=(
            P("row", "col"),
            P("row", "col"),
            P(),
            P("row", None),
            P("row", None, None),
            P("col"),
            P("row", "col"),
            P("col", "row"),
            P("col"),
            P("row", "col"),
            P("col", "row", None),
            P("row", "col"),
            P("row", "col"),
            P("col", "row"),
        ),
        out_specs=(
            P("row", "col"),
            P("row", "col"),
            P(("col", "row")),
            P("row", "col"),
            P("col", "row"),
            P(("col", "row")),
            P("row", "col"),
            P("col", "row", None),
            P("row", "col"),
            P("row", "col"),
            P("col", "row"),
        ),
        check_vma=False,
    )
```

time: 1040 us -> 624 us (0.60)
  waiting for transfers between devices: 523 us -> 0 us
  Pallas kernels: 152 us -> 513 us
  blocking collectives: 143 us -> 7.3 us
  other arithmetic: 75.9 us -> 33 us
  local copies, waits for them, and re-layouts: 55.9 us -> 25.5 us
  matrix products: 50.2 us -> 28.1 us
  starting transfers between devices: 17.6 us -> 0 us
    pallas_call x1 -> x9, Pallas kernels: 152 us -> 513 us  [the longest x6 344 us: remote_call(): pl.pallas_call(functools.partial(kernel, rows, cols), out_shape=[jax.Shap...]
    reduce_scatter x9 -> x0, waiting for transfers between devices: 249 us -> none  [the longest x1 51 us: per_device(): lax.psum_scatter(grad_query_w, 'row', scatter_dimension=0, tiled=True)]
    psum x4 -> x0, waiting for transfers between devices: 166 us -> none  [the longest x1 65 us: per_device(): grad_hidden_two = lax.psum(hidden_two_part, 'col')]
    all_gather x6 -> x0, waiting for transfers between devices: 94.5 us -> none  [the longest x1 34.5 us: per_device(): lax.all_gather(jnp.concatenate([pick_weights_low, grad_memory], axis=1),...]
    all_gather x7 -> x1, blocking collectives: 91.1 us -> 7.3 us  [per_device(): lax.all_gather(norm1_gain.astype(LOW), 'col', axis=0, tiled=True)]
    unnamed x1 -> x0, blocking collectives: 33.4 us -> none
    reduce_sum x10 -> x5, other arithmetic: 37 us -> 4 us  [the longest x1 1.72 us: per_device(): send_pos = jnp.sum(jnp.where(mine, slot_pos[None, :], 0), axis=1)]
    dot_general x24 -> x18, matrix products: 50.2 us -> 28.1 us  [the longest x1 3.29 us: attention_backward(): jnp.einsum('qhd,khd->hqk', grad_out, value_rows, preferred_element_type=F32)]
  transfers between devices with their start and end apart: 22 -> 0, of which waited for: 16 -> 0; matrix products, arithmetic and copies ran while one was open for 12% -> 0% of each run, Pallas kernels for 0% -> 0%
where the time goes in v2:
time: 624 us; the launch traced here: 613 us
  Pallas kernels  513 us (82%)
  other arithmetic  33 us (5%)
  matrix products  28.1 us (5%)
  local copies, waits for them, and re-layouts  25.5 us (4%)
  blocking collectives  7.3 us (1%)
    pallas_call x6, Pallas kernels, remote_call(): pl.pallas_call(functools.partial(kernel, rows, cols), out_shape=[jax.Shap...  344 us
    pallas_call x1, Pallas kernels, memory_call(): pl.pallas_call(functools.partial(memory_kernel, groups, block, 4), grid=(...  157 us

profile of v2, /device:TPU:0, one launch (start us, length us, event | category | flops | bytes accessed | tf_op | source)
XLA Modules:
  0.0 613.0 jit_solution(14402016070525831752)
XLA Ops:
  0.7 0.8 fusion.75
  1.4 1.1 reduce-window.30
  2.8 0.8 add_select_fusion.3
  3.7 0.8 multiply_add_fusion
  5.0 0.9 copy.107.recv_col
  5.9 0.7 fusion.44
  6.6 1.1 reduce-window.21
  8.2 0.7 subtract_add_fusion
  8.9 1.7 select_reduce_fusion
  10.7 1.0 convert_element_type.98
  11.7 1.0 copy.106
  12.7 0.7 pad_maximum_fusion.7.shard
  13.4 41.5 %shard_map.221 = (bf16[512,1024]{1,0:T(8,128)(2,1)}, bf16[1024,1024]{1,0:T(8,128)(2,1)}) custom-call(bf16[512,256]{1,0:T(8,128)(2,1)} %tokens_ref.1, s32[1,512]{1,0:T(1,128)} %bitcast.157, s32[512,1]{1,0:T(8,128)} %copy.107.recv_col, bf16[128,1024]{1,0:T(8,128)(2,1)} %pad_maximum_fusion.7.shard), custom_call_target="tpu_custom_call" | custom-call | tf_op jit(solution)/shard_map/pallas_call | solution.py:499
  54.9 1.5 multiply_reduce_fusion.1
  57.0 7.3 %all-gather = bf16[4,1,256]{2,1,0:T(2,128)(2,1)S(1)} all-gather(bf16[1,1,256]{2,1,0:T(2,128)(2,1)S(1)} %reshape.193), channel_id=1, replica_groups=mesh['row'=8,'col'=4] {'col'}, dimensions={0}, use_global_device_ids=true | all-gather | bytes 2560 | tf_op jit(solution)/shard_map/all_gather | solution.py:773
  64.3 2.8 convolution_convert_fusion.1
  67.9 0.9 fusion.55
  69.5 1.1 copy-done.26
  70.5 0.8 fusion.16
  72.1 2.8 fusion.30.part
  75.2 0.8 constant_dynamic-slice_fusion.4.dealt
  76.0 1.3 convert_convert_fusion
  77.3 1.1 convert_element_type.110
  78.5 0.9 convert_element_type.111
  79.4 0.8 pad_maximum_fusion.6.shard
  80.2 0.8 copy.115.picks
  81.6 76.1 %shard_map.222 = (bf16[512,1024]{1,0:T(8,128)(2,1)}, f32[512,256]{1,0:T(8,128)}, f32[512,128]{1,0:T(8,128)}, bf16[512,1024]{1,0:T(8,128)(2,1)}, bf16[1024,1536]{...) custom-call(f32[512,1024]{1,0:T(8,128)} %fusion.30.part, ...), custom_call_target="tpu_custom_call" | custom-call | tf_op jit(solution)/shard_map/pallas_call | solution.py:499
  163.9 0.7 pad.4.clone.index
  164.6 5.9 shard_map.223
  170.6 41.0 %shard_map.224 = (f32[128,512]{1,0:T(8,128)}, bf16[8,128,512]{2,1,0:T(8,128)(2,1)}, bf16[4096,256]{1,0:T(8,128)(2,1)}) custom-call(f32[64,512]{1,0:T(8,128)} %get-tuple-element.48.part, bf16[512,256]{1,0:T(8,128)(2,1)} %get-tuple-element.49.grads), custom_call_target="tpu_custom_call" | custom-call | tf_op jit(solution)/shard_map/pallas_call | solution.py:499
  211.5 5.8 convert_element_type.116.table_ref
  217.4 156.7 %shard_map.225 = (f32[4096,256]{1,0:T(8,128)}, f32[8,128,512]{2,1,0:T(8,128)}, f32[8192,256]{1,0:T(8,128)}) custom-call(s16[4096,128]{1,0:T(8,128)(2,1)} %get-tuple-element.51.picks_ref, bf16[8,128,512]{2,1,0:T(8,128)(2,1)} %get-tuple-element.52.w_ref, bf16[4096,256]{1,0:T(8,128)(2,1)} %get-tuple-element.53.dm_ref, ...), custom_call_target="tpu_custom_call" | custom-call | tf_op jit(solution)/shard_map/pallas_call | solution.py:669
  374.1 41.2 %shard_map.226 = (f32[512,256]{1,0:T(8,128)}, f32[32,512]{1,0:T(8,128)}) custom-call(f32[4096,256]{1,0:T(8,128)} %get-tuple-element.54.mem_part, f32[8,128,512]{2,1,0:T(8,128)} %get-tuple-element.55.dw_part), custom_call_target="tpu_custom_call" | custom-call | tf_op jit(solution)/shard_map/pallas_call | solution.py:499
  415.3 1.5 constant_dynamic-slice_fusion.3.weights
  416.9 6.2 %shard_map.227 = bf16[512,512]{1,0:T(8,128)(2,1)} custom-call(f32[32,512]{1,0:T(8,128)} %constant_dynamic-slice_fusion.3.weights, f32[32,512]{1,0:T(8,128)} %get-tuple-element.56.dw, s32[64,512]{1,0:T(8,128)} %get-tuple-element.125.index), custom_call_target="tpu_custom_call" | custom-call | tf_op jit(solution)/shard_map/pallas_call | solution.py:513
  423.0 1.3 copy.145
  424.3 1.4 fusion.22.key_grad
  426.3 0.9 multiply_convert_fusion.2
  427.2 1.8 copy.119
  429.0 2.6 fusion.26
  432.1 3.6 pad_maximum_fusion.weight_grad
  435.8 1.8 fusion.27.result_part
  437.6 2.9 fusion.2.part
  440.5 0.7 constant_dynamic-slice_fusion.2.cot
  441.2 0.9 copy.123.send_col
  442.1 87.2 %shard_map.228 = (bf16[512,1024]{1,0:T(8,128)(2,1)}, f32[512,256]{1,0:T(8,128)}, f32[512,256]{1,0:T(8,128)}, f32[128,1536]{1,0:T(8,128)}, f32[2,32,512]{2,1,0:T(8,128)}, /*index=5*/f32[8,256]{1,0:T(8,128)}) custom-call(f32[512,1024]{1,0:T(8,128)} %fusion.2.part, f32[512,1024]{1,0:T(8,128)} %fusion.27.result_part, f32[512,256]{1,0:T(8,128)} %get-tuple-element.60.resid, ...), custom_call_target="tpu_custom_call" | custom-call | tf_op jit(solution)/shard_map/pallas_call | solution.py:499
  529.3 1.7 convolution_convert_fusion.2
  531.1 3.3 multiply_reduce_fusion
  534.5 1.2 multiply_convert_fusion
  536.2 0.8 fusion.17
  537.0 0.8 fusion.19
  538.0 1.2 fusion.32
  539.7 2.6 pad_maximum_fusion.1.weight_grad
  542.3 2.4 fusion.8.part
  544.6 0.8 broadcast_in_dim.83.factor
  545.5 57.3 %shard_map.229 = (f32[512,256]{1,0:T(8,128)}, f32[128,1024]{1,0:T(8,128)}, f32[8,256]{1,0:T(8,128)}) custom-call(f32[512,1024]{1,0:T(8,128)} %fusion.8.part, f32[512,256]{1,0:T(8,128)} %constant_dynamic-slice_fusion.4.dealt, f32[512,128]{1,0:T(8,128)} %broadcast_in_dim.83.factor, f32[1,256]{1,0:T(1,128)} %bitcast.165, f32[512,256]{1,0:T(8,128)} %get-tuple-element.65.extra, ...), custom_call_target="tpu_custom_call" | custom-call | tf_op jit(solution)/shard_map/pallas_call | solution.py:499
  602.8 1.9 slice.75
  604.7 0.9 slice_bitcast_fusion.10
  605.6 0.8 copy.131
  606.4 0.8 fusion.53
  608.3 0.8 slice.78
  609.8 0.8 copy.132
  610.6 0.8 copy.155
  611.4 0.8 copy.156
  (105 shorter events, 11.3 us)
Async XLA Ops:
  0.6 55.8 %copy-start.29 = (f32[256]{0:T(256)S(1)}, f32[256]{0:T(256)}, u32[]{:S(2)}) copy-start(f32[256]{0:T(256)} %param.19) | copy-start | bytes 3076
  4.5 0.5 copy-start.28
  64.3 3.1 copy-start.30
  67.4 2.0 copy-start.6
  68.8 2.6 copy-start
  69.4 1.1 copy-start.26
  71.4 0.7 copy-start.11
  71.4 3.5 copy-start.2
  74.9 3.4 copy-start.21
  74.9 5.2 copy-start.15
  76.0 5.0 copy-start.22
  374.1 50.3 %copy-start.9 = (bf16[512,1024]{1,0:T(8,128)(2,1)S(1)}, bf16[512,1024]{1,0:T(8,128)(2,1)}, u32[]{:S(2)}) copy-start(bf16[512,1024]{1,0:T(8,128)(2,1)} %get-tuple-element.62) | copy-start | bytes 3145732
  415.3 10.4 %copy-start.8 = (bf16[2,256,512]{2,1,0:T(8,128)(2,1)S(1)}, bf16[2,256,512]{2,1,0:T(8,128)(2,1)}, u32[]{:S(2)}) copy-start(bf16[2,256,512]{2,1,0:T(8,128)(2,1)} %get-tuple-element.44.keys) | copy-start | bytes 1572868
  424.3 2.0 copy-start.18
  424.3 2.0 copy-start.19
  424.3 2.0 copy-start.20
  426.2 2.8 copy-start.5
  429.0 2.6 copy-start.3
  432.1 3.6 copy-start.4
  435.8 1.8 copy-start.13
  437.6 3.6 copy-start.25
  442.1 87.3 %copy-start.24 = (bf16[1024,1024]{1,0:T(8,128)(2,1)S(1)}, bf16[1024,1024]{1,0:T(8,128)(2,1)}, u32[]{:S(2)}) copy-start(bf16[1024,1024]{1,0:T(8,128)(2,1)} %get-tuple-element.43) | copy-start | bytes 6291460
  442.1 89.0 %copy-start.27 = (f32[4,512]{1,0:T(4,128)S(1)}, f32[4,512]{1,0:T(4,128)}, u32[]{:S(2)}) copy-start(f32[4,512]{1,0:T(4,128)} %copy-done.26) | copy-start | bytes 24580
  442.1 89.0 %copy-start.7 = (bf16[512,768]{0,1:T(8,128)(2,1)S(1)}, bf16[512,768]{0,1:T(8,128)(2,1)}, u32[]{:S(2)}) copy-start(bf16[512,768]{0,1:T(8,128)(2,1)} %copy-done.6) | copy-start | bytes 2359300
  531.1 3.5 copy-start.1
  537.9 1.2 copy-start.10
  537.9 1.3 copy-start.12
  545.5 62.8 %copy-start.14 = (f32[128,1536]{1,0:T(8,128)S(1)}, f32[128,1536]{1,0:T(8,128)}, u32[]{:S(2)}) copy-start(f32[128,1536]{1,0:T(8,128)} %get-tuple-element.70) | copy-start | bytes 2359300
  602.8 7.8 %copy-start.16 = (f32[512,256]{1,0:T(8,128)S(1)}, f32[512,256]{1,0:T(8,128)}, u32[]{:S(2)}) copy-start(f32[512,256]{1,0:T(8,128)} %get-tuple-element.148) | copy-start | bytes 1572868
  602.8 8.5 %copy-start.17 = (f32[512,256]{1,0:T(8,128)S(1)}, f32[512,256]{1,0:T(8,128)}, u32[]{:S(2)}) copy-start(f32[512,256]{1,0:T(8,128)} %get-tuple-element.149) | copy-start | bytes 1572868
  602.8 9.3 %copy-start.23 = (f32[2,32,512]{2,1,0:T(8,128)S(1)}, f32[2,32,512]{2,1,0:T(8,128)}, u32[]{:S(2)}) copy-start(f32[2,32,512]{2,1,0:T(8,128)} %get-tuple-element.155) | copy-start | bytes 393220
